TPU v7x, 32 devices: a whole 2x2x4 slice. The times are simulated.
32 devices in a mesh: prod: 4 (over y, core), draw: 8 (over z, x).
Axes of the slice: x: 2, y: 2, z: 4, core: 2. Of those that a mesh axis runs over, the one named last changes fastest.
Arguments:
- product_traits: float32 [32, 262144], P(None, 'prod'), may hold values from -4 to 4
- mean_utility: float32 [262144], P('prod'), may hold values from -3 to 3
- target: float32 [262144], P('prod'), may hold values from -3 to 3
- taste_scale: float32 [32], replicated, may hold values from 0.02 to 0.2
- taste_draws: float32 [32, 2048], P(None, 'draw'), may hold values from -4 to 4
- outside: float32 [4, 2048], P(None, 'draw'), may hold values from -3 to 3
- block_market: int32 [1024], P('prod'), may hold values from 0 to 3
Outputs:
- mean_level: float32 [262144], P(('prod', 'draw'))
- residual: float32 [262144], P(('prod', 'draw'))
All inputs are finite; a program needn't handle non-finite values.
Results may differ from a plain program's by a relative error of at most 0.0003.
Values sent between devices are 32-bit elements; how exact they have to be, the bound alone decides.
No kernel may reach another device: no remote copies, remote signals or barrier semaphores. Data moves between devices by JAX's collectives and lax.ppermute only.
A program may use at most 192 MiB of HBM per device.

v0:
```python
import jax
import jax.numpy as jnp
from jax import lax
from jax.sharding import PartitionSpec as P

MARKETS = 4
BLOCK = 256
ITERS = 2


def exp_tile(product_traits, level_now, taste_mix, tile_index, tile_len):
    start = tile_index * tile_len
    columns = lax.dynamic_slice_in_dim(product_traits, start, tile_len, 1)
    levels = lax.dynamic_slice_in_dim(level_now, start, tile_len, 0)
    spread = jnp.dot(
        taste_mix.T, columns, precision=lax.Precision.HIGHEST, preferred_element_type=jnp.float32
    )
    return jnp.exp(levels[None, :] + spread)


def market_sums(expo_tile, onehot_tile):
    draws_here = expo_tile.shape[0]
    block_count = onehot_tile.shape[0]
    block_sums = expo_tile.reshape(draws_here, block_count, BLOCK).sum(axis=2)
    return jnp.dot(block_sums, onehot_tile, precision=lax.Precision.HIGHEST)


def share_tile(expo_tile, onehot_tile, inverse):
    draws_here = expo_tile.shape[0]
    block_count = onehot_tile.shape[0]
    per_block = jnp.dot(inverse, onehot_tile.T, precision=lax.Precision.HIGHEST)
    shaped = expo_tile.reshape(draws_here, block_count, BLOCK)
    return jnp.einsum("rnb,rn->nb", shaped, per_block, precision=lax.Precision.HIGHEST).reshape(-1)


def body(product_traits, mean_utility, target, taste_scale, taste_draws, outside, block_market):
    prod_count = product_traits.shape[1]
    draw_count = taste_draws.shape[1]
    draw_devices = lax.axis_size("draw")
    market_scale = float(prod_count * lax.axis_size("prod") // MARKETS)
    total_draws = float(draw_count * draw_devices)
    tile_len = min(8192, prod_count)
    tile_count = prod_count // tile_len
    blocks_tile = tile_len // BLOCK
    taste_mix = taste_scale[:, None] * taste_draws
    onehot = (block_market[:, None] == jnp.arange(MARKETS, dtype=jnp.int32)[None, :]).astype(
        jnp.float32
    )
    onehot_tiles = onehot.reshape(tile_count, blocks_tile, MARKETS)
    outside_term = (market_scale * jnp.exp(outside)).T
    part_len = prod_count // draw_devices
    own_start = lax.axis_index("draw") * part_len
    tile_ids = jnp.arange(tile_count, dtype=jnp.int32)
    mean_level = mean_utility
    level_part = lax.dynamic_slice_in_dim(mean_level, own_start, part_len, 0)
    residual_part = jnp.zeros_like(level_part)
    for sweep_index in range(ITERS):
        level_now = mean_level
        stored = lax.map(
            lambda tile_index: exp_tile(product_traits, level_now, taste_mix, tile_index, tile_len),
            tile_ids,
        )
        local_sums = jnp.sum(jax.vmap(market_sums)(stored, onehot_tiles), axis=0)
        denominator = lax.psum(local_sums, "prod") + outside_term
        inverse = 1.0 / denominator
        shares = lax.map(
            lambda tile_pair: share_tile(tile_pair[0], tile_pair[1], inverse),
            (stored, onehot_tiles),
        ).reshape(-1)
        local_share = shares / total_draws
        share_full = lax.psum(local_share, "draw")
        residual_full = target - jnp.log(market_scale * share_full)
        mean_level = mean_level + residual_full
        residual_part = lax.dynamic_slice_in_dim(residual_full, own_start, part_len, 0)
        level_part = lax.dynamic_slice_in_dim(mean_level, own_start, part_len, 0)
    return (level_part, residual_part)


def solution(mesh):
    placed = (
        P(None, "prod"),
        P("prod"),
        P("prod"),
        P(),
        P(None, "draw"),
        P(None, "draw"),
        P("prod"),
    )
    return jax.shard_map(
        body,
        mesh=mesh,
        in_specs=placed,
        out_specs=(P(("prod", "draw")), P(("prod", "draw"))),
        check_vma=False,
    )
```

profile of v0, /device:TPU:0, one launch (start us, length us, event | category | flops | bytes accessed | tf_op | source)
XLA Modules:
  0.0 646.6 jit_solution(3625412685054337435)
XLA Ops:
  8.0 21.0 %broadcast.36.clone = f32[8,256,8192]{1,2,0:T(8,128)} broadcast(f32[]{:T(128)} %constant.60.clone.1), dimensions={} | broadcast | bytes 67108864 | tf_op jit(solution)/shard_map/broadcast.9
  29.1 102.0 %while.40 = (s32[]{:T(128)}, f32[8,256,8192]{1,2,0:T(8,128)}, s32[8]{0:T(128)S(1)}, f32[65536]{0:T(1024)S(1)}, f32[32,65536]{1,0:T(8,128)}, /*index=5*/f32[32,25...) while((s32[]{:T(128)}, f32[8,256,8192]{1,2,0:T(8,128)}, s32[8]{0:T(128)S(1)}, ...), condition=%wide.region_1.2_spmd, body=%wide.region_0.1_spmd.sunk | while | flops 807403520 | bytes 9568935 | solution.py:59
  30.2 11.6 %fusion.51 = f32[8,256,8192]{1,2,0:T(8,128)} fusion(f32[8,256,8192]{1,2,0:T(8,128)} %get-tuple-element.327, s32[]{:T(128)} %get-tuple-element.326, f32[32,256]{1,0:T(8,128)S(1)} %get-tuple-element.341, f32[8192]{0:T(1024)S(1)} %dynamic_slice.71, f32[32,65536]{1,0:T(8,128)} %get-tuple-element.340, s32[]{:T(128)S(6)} %select_n.15), kind=kOutput, calls=%fused_computation.3.clone.1 | convolution fusion | flops 807403520 | bytes 9503236 | tf_op jit(solution)/shard_map/while/body/eval_jaxpr/dot_general | solution.py:15
  43.0 11.6 %fusion.51 = f32[8,256,8192]{1,2,0:T(8,128)} fusion(f32[8,256,8192]{1,2,0:T(8,128)} %get-tuple-element.327, s32[]{:T(128)} %get-tuple-element.326, f32[32,256]{1,0:T(8,128)S(1)} %get-tuple-element.341, f32[8192]{0:T(1024)S(1)} %dynamic_slice.71, f32[32,65536]{1,0:T(8,128)} %get-tuple-element.340, s32[]{:T(128)S(6)} %select_n.15), kind=kOutput, calls=%fused_computation.3.clone.1 | convolution fusion | flops 807403520 | bytes 9503236 | tf_op jit(solution)/shard_map/while/body/eval_jaxpr/dot_general | solution.py:15
  55.7 11.6 %fusion.51 = f32[8,256,8192]{1,2,0:T(8,128)} fusion(f32[8,256,8192]{1,2,0:T(8,128)} %get-tuple-element.327, s32[]{:T(128)} %get-tuple-element.326, f32[32,256]{1,0:T(8,128)S(1)} %get-tuple-element.341, f32[8192]{0:T(1024)S(1)} %dynamic_slice.71, f32[32,65536]{1,0:T(8,128)} %get-tuple-element.340, s32[]{:T(128)S(6)} %select_n.15), kind=kOutput, calls=%fused_computation.3.clone.1 | convolution fusion | flops 807403520 | bytes 9503236 | tf_op jit(solution)/shard_map/while/body/eval_jaxpr/dot_general | solution.py:15
  68.5 11.6 %fusion.51 = f32[8,256,8192]{1,2,0:T(8,128)} fusion(f32[8,256,8192]{1,2,0:T(8,128)} %get-tuple-element.327, s32[]{:T(128)} %get-tuple-element.326, f32[32,256]{1,0:T(8,128)S(1)} %get-tuple-element.341, f32[8192]{0:T(1024)S(1)} %dynamic_slice.71, f32[32,65536]{1,0:T(8,128)} %get-tuple-element.340, s32[]{:T(128)S(6)} %select_n.15), kind=kOutput, calls=%fused_computation.3.clone.1 | convolution fusion | flops 807403520 | bytes 9503236 | tf_op jit(solution)/shard_map/while/body/eval_jaxpr/dot_general | solution.py:15
  81.2 11.6 %fusion.51 = f32[8,256,8192]{1,2,0:T(8,128)} fusion(f32[8,256,8192]{1,2,0:T(8,128)} %get-tuple-element.327, s32[]{:T(128)} %get-tuple-element.326, f32[32,256]{1,0:T(8,128)S(1)} %get-tuple-element.341, f32[8192]{0:T(1024)S(1)} %dynamic_slice.71, f32[32,65536]{1,0:T(8,128)} %get-tuple-element.340, s32[]{:T(128)S(6)} %select_n.15), kind=kOutput, calls=%fused_computation.3.clone.1 | convolution fusion | flops 807403520 | bytes 9503236 | tf_op jit(solution)/shard_map/while/body/eval_jaxpr/dot_general | solution.py:15
  94.0 11.6 %fusion.51 = f32[8,256,8192]{1,2,0:T(8,128)} fusion(f32[8,256,8192]{1,2,0:T(8,128)} %get-tuple-element.327, s32[]{:T(128)} %get-tuple-element.326, f32[32,256]{1,0:T(8,128)S(1)} %get-tuple-element.341, f32[8192]{0:T(1024)S(1)} %dynamic_slice.71, f32[32,65536]{1,0:T(8,128)} %get-tuple-element.340, s32[]{:T(128)S(6)} %select_n.15), kind=kOutput, calls=%fused_computation.3.clone.1 | convolution fusion | flops 807403520 | bytes 9503236 | tf_op jit(solution)/shard_map/while/body/eval_jaxpr/dot_general | solution.py:15
  106.7 11.6 %fusion.51 = f32[8,256,8192]{1,2,0:T(8,128)} fusion(f32[8,256,8192]{1,2,0:T(8,128)} %get-tuple-element.327, s32[]{:T(128)} %get-tuple-element.326, f32[32,256]{1,0:T(8,128)S(1)} %get-tuple-element.341, f32[8192]{0:T(1024)S(1)} %dynamic_slice.71, f32[32,65536]{1,0:T(8,128)} %get-tuple-element.340, s32[]{:T(128)S(6)} %select_n.15), kind=kOutput, calls=%fused_computation.3.clone.1 | convolution fusion | flops 807403520 | bytes 9503236 | tf_op jit(solution)/shard_map/while/body/eval_jaxpr/dot_general | solution.py:15
  119.5 11.6 %fusion.51 = f32[8,256,8192]{1,2,0:T(8,128)} fusion(f32[8,256,8192]{1,2,0:T(8,128)} %get-tuple-element.327, s32[]{:T(128)} %get-tuple-element.326, f32[32,256]{1,0:T(8,128)S(1)} %get-tuple-element.341, f32[8192]{0:T(1024)S(1)} %dynamic_slice.71, f32[32,65536]{1,0:T(8,128)} %get-tuple-element.340, s32[]{:T(128)S(6)} %select_n.15), kind=kOutput, calls=%fused_computation.3.clone.1 | convolution fusion | flops 807403520 | bytes 9503236 | tf_op jit(solution)/shard_map/while/body/eval_jaxpr/dot_general | solution.py:15
  131.0 20.7 %bitcast_reduce_fusion.1 = f32[8,256,32]{1,2,0:T(8,128)S(1)} fusion(f32[8,256,8192]{1,2,0:T(8,128)} %get-tuple-element.348), kind=kLoop, calls=%fused_computation.29 | loop fusion | flops 16711680 | bytes 67371008 | tf_op jit(solution)/shard_map/vmap()/reduce_sum | solution.py:24
  152.0 8.4 %psum.28 = f32[256,4]{0,1:T(4,128)S(1)} all-reduce(f32[256,4]{0,1:T(4,128)S(1)} %convolution_bitcast_fusion.3), channel_id=1, replica_groups=mesh['prod'=4,'draw'=8] {'prod'}, use_global_device_ids=true, to_apply=%region_3.4 | all-reduce | flops 1024 | bytes 8192 | tf_op jit(solution)/shard_map/psum | solution.py:64
  160.4 92.1 %while.41 = (s32[]{:T(128)}, f32[8,8192]{1,0:T(8,128)S(1)}, f32[8,256,8192]{1,2,0:T(8,128)}, f32[8,32,4]{1,2,0:T(4,128)S(1)}, f32[256,4]{0,1:T(4,128)S(1)}, /*index=5*/s32[]{:T(128)}, s32[]{:T(128)}) while((s32[]{:T(128)}, f32[8,8192]{1,0:T(8,128)S(1)}, f32[8,256,8192]{1,2,0:T(8,128)}, f32[8,32,4]{1,2,0:T(4,128)S(1)}, f32[256,4]{0,1:T(4,128)S(1)}, ...), condition=%wide.region_5.6_spmd, body=%wide.region_4.5_spmd.sunk | while | flops 25559040 | bytes 25466968 | solution.py:66
  253.4 71.0 %all-reduce.3.cloned.1.call-done = f32[65536]{0:T(1024)} async-done(((f32[65536]{0:T(1024)}), f32[65536]{0:T(1024)}) %all-reduce.3.cloned.1.call-update) | async-done | bytes 262160 | tf_op jit(solution)/shard_map/psum | solution.py:71
  325.3 21.0 %broadcast.36 = f32[8,256,8192]{1,2,0:T(8,128)} broadcast(f32[]{:T(128)} %constant.60.clone.1), dimensions={} | broadcast | bytes 67108864 | tf_op jit(solution)/shard_map/broadcast.9
  346.3 102.0 %while.42 = (s32[]{:T(128)}, f32[8,256,8192]{1,2,0:T(8,128)}, s32[8]{0:T(128)S(1)}, f32[65536]{0:T(1024)S(1)}, f32[32,65536]{1,0:T(8,128)}, /*index=5*/f32[32,25...) while((s32[]{:T(128)}, f32[8,256,8192]{1,2,0:T(8,128)}, s32[8]{0:T(128)S(1)}, ...), condition=%wide.region_8.9_spmd, body=%wide.region_7.8_spmd.sunk | while | flops 807403520 | bytes 9568935 | solution.py:59
  347.5 11.6 %fusion.59 = f32[8,256,8192]{1,2,0:T(8,128)} fusion(f32[8,256,8192]{1,2,0:T(8,128)} %get-tuple-element.378, s32[]{:T(128)} %get-tuple-element.377, f32[32,256]{1,0:T(8,128)S(1)} %get-tuple-element.392, f32[8192]{0:T(1024)S(1)} %dynamic_slice.76, f32[32,65536]{1,0:T(8,128)} %get-tuple-element.391, s32[]{:T(128)S(6)} %select_n.16), kind=kOutput, calls=%fused_computation.17.clone.1 | convolution fusion | flops 807403520 | bytes 9503236 | tf_op jit(solution)/shard_map/while/body/eval_jaxpr/dot_general | solution.py:15
  360.3 11.6 %fusion.59 = f32[8,256,8192]{1,2,0:T(8,128)} fusion(f32[8,256,8192]{1,2,0:T(8,128)} %get-tuple-element.378, s32[]{:T(128)} %get-tuple-element.377, f32[32,256]{1,0:T(8,128)S(1)} %get-tuple-element.392, f32[8192]{0:T(1024)S(1)} %dynamic_slice.76, f32[32,65536]{1,0:T(8,128)} %get-tuple-element.391, s32[]{:T(128)S(6)} %select_n.16), kind=kOutput, calls=%fused_computation.17.clone.1 | convolution fusion | flops 807403520 | bytes 9503236 | tf_op jit(solution)/shard_map/while/body/eval_jaxpr/dot_general | solution.py:15
  373.0 11.6 %fusion.59 = f32[8,256,8192]{1,2,0:T(8,128)} fusion(f32[8,256,8192]{1,2,0:T(8,128)} %get-tuple-element.378, s32[]{:T(128)} %get-tuple-element.377, f32[32,256]{1,0:T(8,128)S(1)} %get-tuple-element.392, f32[8192]{0:T(1024)S(1)} %dynamic_slice.76, f32[32,65536]{1,0:T(8,128)} %get-tuple-element.391, s32[]{:T(128)S(6)} %select_n.16), kind=kOutput, calls=%fused_computation.17.clone.1 | convolution fusion | flops 807403520 | bytes 9503236 | tf_op jit(solution)/shard_map/while/body/eval_jaxpr/dot_general | solution.py:15
  385.8 11.6 %fusion.59 = f32[8,256,8192]{1,2,0:T(8,128)} fusion(f32[8,256,8192]{1,2,0:T(8,128)} %get-tuple-element.378, s32[]{:T(128)} %get-tuple-element.377, f32[32,256]{1,0:T(8,128)S(1)} %get-tuple-element.392, f32[8192]{0:T(1024)S(1)} %dynamic_slice.76, f32[32,65536]{1,0:T(8,128)} %get-tuple-element.391, s32[]{:T(128)S(6)} %select_n.16), kind=kOutput, calls=%fused_computation.17.clone.1 | convolution fusion | flops 807403520 | bytes 9503236 | tf_op jit(solution)/shard_map/while/body/eval_jaxpr/dot_general | solution.py:15
  398.6 11.6 %fusion.59 = f32[8,256,8192]{1,2,0:T(8,128)} fusion(f32[8,256,8192]{1,2,0:T(8,128)} %get-tuple-element.378, s32[]{:T(128)} %get-tuple-element.377, f32[32,256]{1,0:T(8,128)S(1)} %get-tuple-element.392, f32[8192]{0:T(1024)S(1)} %dynamic_slice.76, f32[32,65536]{1,0:T(8,128)} %get-tuple-element.391, s32[]{:T(128)S(6)} %select_n.16), kind=kOutput, calls=%fused_computation.17.clone.1 | convolution fusion | flops 807403520 | bytes 9503236 | tf_op jit(solution)/shard_map/while/body/eval_jaxpr/dot_general | solution.py:15
  411.3 11.6 %fusion.59 = f32[8,256,8192]{1,2,0:T(8,128)} fusion(f32[8,256,8192]{1,2,0:T(8,128)} %get-tuple-element.378, s32[]{:T(128)} %get-tuple-element.377, f32[32,256]{1,0:T(8,128)S(1)} %get-tuple-element.392, f32[8192]{0:T(1024)S(1)} %dynamic_slice.76, f32[32,65536]{1,0:T(8,128)} %get-tuple-element.391, s32[]{:T(128)S(6)} %select_n.16), kind=kOutput, calls=%fused_computation.17.clone.1 | convolution fusion | flops 807403520 | bytes 9503236 | tf_op jit(solution)/shard_map/while/body/eval_jaxpr/dot_general | solution.py:15
  424.1 11.6 %fusion.59 = f32[8,256,8192]{1,2,0:T(8,128)} fusion(f32[8,256,8192]{1,2,0:T(8,128)} %get-tuple-element.378, s32[]{:T(128)} %get-tuple-element.377, f32[32,256]{1,0:T(8,128)S(1)} %get-tuple-element.392, f32[8192]{0:T(1024)S(1)} %dynamic_slice.76, f32[32,65536]{1,0:T(8,128)} %get-tuple-element.391, s32[]{:T(128)S(6)} %select_n.16), kind=kOutput, calls=%fused_computation.17.clone.1 | convolution fusion | flops 807403520 | bytes 9503236 | tf_op jit(solution)/shard_map/while/body/eval_jaxpr/dot_general | solution.py:15
  436.8 11.6 %fusion.59 = f32[8,256,8192]{1,2,0:T(8,128)} fusion(f32[8,256,8192]{1,2,0:T(8,128)} %get-tuple-element.378, s32[]{:T(128)} %get-tuple-element.377, f32[32,256]{1,0:T(8,128)S(1)} %get-tuple-element.392, f32[8192]{0:T(1024)S(1)} %dynamic_slice.76, f32[32,65536]{1,0:T(8,128)} %get-tuple-element.391, s32[]{:T(128)S(6)} %select_n.16), kind=kOutput, calls=%fused_computation.17.clone.1 | convolution fusion | flops 807403520 | bytes 9503236 | tf_op jit(solution)/shard_map/while/body/eval_jaxpr/dot_general | solution.py:15
  448.4 20.7 %bitcast_reduce_fusion = f32[8,256,32]{1,2,0:T(8,128)S(1)} fusion(f32[8,256,8192]{1,2,0:T(8,128)} %get-tuple-element.399), kind=kLoop, calls=%fused_computation.28 | loop fusion | flops 16711680 | bytes 67371008 | tf_op jit(solution)/shard_map/vmap()/reduce_sum | solution.py:24
  475.0 92.1 %while.43 = (s32[]{:T(128)}, f32[8,8192]{1,0:T(8,128)S(1)}, f32[8,256,8192]{1,2,0:T(8,128)}, f32[8,32,4]{1,2,0:T(4,128)S(1)}, f32[256,4]{0,1:T(4,128)S(1)}, /*index=5*/s32[]{:T(128)}, s32[]{:T(128)}) while((s32[]{:T(128)}, f32[8,8192]{1,0:T(8,128)S(1)}, f32[8,256,8192]{1,2,0:T(8,128)}, f32[8,32,4]{1,2,0:T(4,128)S(1)}, ...), condition=%wide.region_12.13_spmd, body=%wide.region_11.12_spmd.sunk | while | flops 25559040 | bytes 25466968 | solution.py:66
  479.2 7.1 %fusion.64 = f32[32,1,256]{2,1,0:T(1,128)S(1)} fusion(f32[256,32,256]{0,2,1:T(8,128)S(1)} %bitcast.112, f32[256,32,1]{0,1,2:T(8,128)S(1)} %convolution_bitcast_fusion.7), kind=kOutput, calls=%fused_computation.22.clone.1 | convolution fusion | flops 25165824 | bytes 8454144 | tf_op jit(solution)/shard_map/while/body/eval_jaxpr/rnb,rn->nb/dot_general | solution.py:33
  490.7 7.1 %fusion.64 = f32[32,1,256]{2,1,0:T(1,128)S(1)} fusion(f32[256,32,256]{0,2,1:T(8,128)S(1)} %bitcast.112, f32[256,32,1]{0,1,2:T(8,128)S(1)} %convolution_bitcast_fusion.7), kind=kOutput, calls=%fused_computation.22.clone.1 | convolution fusion | flops 25165824 | bytes 8454144 | tf_op jit(solution)/shard_map/while/body/eval_jaxpr/rnb,rn->nb/dot_general | solution.py:33
  502.2 7.1 %fusion.64 = f32[32,1,256]{2,1,0:T(1,128)S(1)} fusion(f32[256,32,256]{0,2,1:T(8,128)S(1)} %bitcast.112, f32[256,32,1]{0,1,2:T(8,128)S(1)} %convolution_bitcast_fusion.7), kind=kOutput, calls=%fused_computation.22.clone.1 | convolution fusion | flops 25165824 | bytes 8454144 | tf_op jit(solution)/shard_map/while/body/eval_jaxpr/rnb,rn->nb/dot_general | solution.py:33
  513.7 7.1 %fusion.64 = f32[32,1,256]{2,1,0:T(1,128)S(1)} fusion(f32[256,32,256]{0,2,1:T(8,128)S(1)} %bitcast.112, f32[256,32,1]{0,1,2:T(8,128)S(1)} %convolution_bitcast_fusion.7), kind=kOutput, calls=%fused_computation.22.clone.1 | convolution fusion | flops 25165824 | bytes 8454144 | tf_op jit(solution)/shard_map/while/body/eval_jaxpr/rnb,rn->nb/dot_general | solution.py:33
  525.2 7.1 %fusion.64 = f32[32,1,256]{2,1,0:T(1,128)S(1)} fusion(f32[256,32,256]{0,2,1:T(8,128)S(1)} %bitcast.112, f32[256,32,1]{0,1,2:T(8,128)S(1)} %convolution_bitcast_fusion.7), kind=kOutput, calls=%fused_computation.22.clone.1 | convolution fusion | flops 25165824 | bytes 8454144 | tf_op jit(solution)/shard_map/while/body/eval_jaxpr/rnb,rn->nb/dot_general | solution.py:33
  567.9 70.2 %all-reduce.5.cloned.1.call-done = f32[65536]{0:T(1024)} async-done(((f32[65536]{0:T(1024)}), f32[65536]{0:T(1024)}) %all-reduce.5.cloned.1.call-update) | async-done | bytes 262160 | tf_op jit(solution)/shard_map/psum | solution.py:71
  (154 shorter events, 168.7 us)
Async XLA Ops:
  7.2 317.1 %all-reduce.3.cloned.1.call-start = ((), (), s32[]{:S(2)}) async-start(), calls=%async_computation | async-start | bytes 524288 | tf_op jit(solution)/shard_map/psum | solution.py:71
  8.0 21.0 %copy-start.1 = (f32[65536]{0:T(1024)S(1)}, f32[65536]{0:T(1024)}, u32[]{:S(2)}) copy-start(f32[65536]{0:T(1024)} %param.16) | copy-start | bytes 786436
  131.0 20.7 %copy-start.3 = (s32[256]{0:T(256)S(1)}, s32[256]{0:T(256)}, u32[]{:S(2)}) copy-start(s32[256]{0:T(256)} %param.21) | copy-start | bytes 3076
  131.0 29.4 %copy-start.2 = (f32[4,256]{1,0:T(4,128)S(1)}, f32[4,256]{1,0:T(4,128)}, u32[]{:S(2)}) copy-start(f32[4,256]{1,0:T(4,128)} %param.20) | copy-start | bytes 12292
  160.4 163.9 %copy-start = (f32[65536]{0:T(1024)S(1)}, f32[65536]{0:T(1024)}, u32[]{:S(2)}) copy-start(f32[65536]{0:T(1024)} %param.17) | copy-start | bytes 786436
  253.3 384.8 %all-reduce.5.cloned.1.call-start = ((), (), s32[]{:S(2)}) async-start(), calls=%async_computation.1 | async-start | bytes 524288 | tf_op jit(solution)/shard_map/psum | solution.py:71
Sparse Core Ops, SparseCore 0:
  253.4 70.8 all-reduce.2
  568.0 70.0 all-reduce.4
where the time goes:
time: 648 us; the launch traced here: 647 us
  matrix products  303 us (47%)
  waiting for transfers between devices  141 us (22%)
  local copies, waits for them, and re-layouts  119 us (18%)
  other arithmetic  44.9 us (7%)
  between operations  14.1 us (2%)
  blocking collectives  14 us (2%)
  loops' own time  9.99 us (2%)
    dot_general x16, matrix products, exp_tile(): jnp.dot(taste_mix.T, columns, precision=lax.Precision.HIGHEST, preferred_...  185 us
    psum x2, waiting for transfers between devices, body(): share_full = lax.psum(local_share, 'draw')  141 us
    dot_general x16, matrix products, share_tile(): jnp.einsum('rnb,rn->nb', shaped, per_block, precision=lax.Precision.HIGHEST)  114 us
    dynamic_slice x16, local copies, waits for them, and re-layouts, body(): lax.map(lambda tile_pair: share_tile(tile_pair[0], tile_pair[1], inverse)...  62.8 us
    another operation x4, local copies, waits for them, and re-layouts  42 us
    reduce_sum x2, other arithmetic, market_sums(): block_sums = expo_tile.reshape(draws_here, block_count, BLOCK).sum(axis=2)  41.4 us
    psum x2, blocking collectives, body(): denominator = lax.psum(local_sums, 'prod') + outside_term  14 us
  transfers between devices with their start and end apart: 2, of which 2 were waited for; matrix products, arithmetic and copies ran while one was open for 0% of the time, Pallas kernels for 0%

commit v1 on v0

v1 whole, which is shorter than its diff:
```python
import functools
import math

import jax
import jax.numpy as jnp
from jax import lax
from jax.experimental import pallas as pl
from jax.experimental.pallas import tpu as pltpu
from jax.sharding import PartitionSpec as P

MARKETS = 4
BLOCK = 256
LANES = 128
HALVES = BLOCK // LANES
LOG2E = math.log2(math.e)
BUDGET = 58 * 2**20
FLOOR = 8 * 2**20
PIECES = 3
STEP_BLOCKS = 32
F32 = jnp.float32
BF16 = jnp.bfloat16
VMEM = pl.BlockSpec(memory_space=pltpu.VMEM)
SMEM = pl.BlockSpec(memory_space=pltpu.SMEM)
ANY = pl.BlockSpec(memory_space=pl.ANY)


def params(*shapes):
    return pltpu.CompilerParams(vmem_limit_bytes=sum(4 * math.prod(shape) for shape in shapes) + 2**20)


def rounded(values):
    return values.astype(BF16).astype(F32)


def top_rows(rows, columns):
    index = lax.broadcasted_iota(jnp.int32, (16, columns), 0)
    tile = jnp.zeros((16, columns), F32)
    for place, row in enumerate(rows):
        tile = jnp.where(index == place, row, tile)
    return tile


def trait_rows(traits, level):
    first = rounded(traits)
    second = traits - first
    scaled = level * LOG2E
    one = rounded(scaled)
    two = rounded(scaled - one)
    three = scaled - one - two
    return [first, second, first, top_rows((one, two, three), traits.shape[1])]


def taste_rows(taste_draws, scale_row):
    k_count, columns = taste_draws.shape
    diagonal = lax.broadcasted_iota(jnp.int32, (k_count, k_count), 0) == lax.broadcasted_iota(
        jnp.int32, (k_count, k_count), 1
    )
    scale = jnp.sum(jnp.where(diagonal, scale_row, 0.0), axis=1, keepdims=True)
    mix = scale * taste_draws * LOG2E
    first = rounded(mix)
    second = mix - first
    one = jnp.ones((1, columns), F32)
    return [first, first, second, top_rows((one, one, one), columns)]


def stacked(rows):
    return jnp.concatenate([row.astype(BF16) for row in rows], axis=0)


def level_row(level_ref, block):
    return jnp.concatenate(
        [level_ref[pl.ds(block * HALVES + half, 1), :] for half in range(HALVES)], axis=1
    )


def mm(left, right):
    return lax.dot_general(left, right, (((1,), (0,)), ((), ())), preferred_element_type=F32)


def first_sums(market_scale, market_ref, traits_ref, level_ref, scale_ref, draws_ref, outside_ref, sums_ref, left, total):
    step = pl.program_id(0)

    @pl.when(step == 0)
    def _():
        rows = jnp.concatenate(taste_rows(draws_ref[...], scale_ref[...]), axis=0)
        left[...] = rows.T.astype(BF16)
        total[...] = jnp.zeros_like(total)

    for local in range(traits_ref.shape[1] // BLOCK):
        block = step * (traits_ref.shape[1] // BLOCK) + local
        right = stacked(
            trait_rows(traits_ref[:, local * BLOCK : (local + 1) * BLOCK], level_row(level_ref, local))
        )
        expo = jnp.exp2(mm(left[...], right))
        part = expo[:, :LANES]
        for half in range(1, HALVES):
            part = part + expo[:, half * LANES : (half + 1) * LANES]
        market = market_ref[block]
        total[market] += part

    @pl.when(step == pl.num_programs(0) - 1)
    def _():
        own = jnp.where(lax.axis_index("prod") == 0, market_scale, 0.0)
        outer = own * jnp.exp(outside_ref[...])
        ones = jnp.ones((8, LANES), F32)
        pieces = []
        for market in range(MARKETS):
            summed = lax.dot_general(
                ones,
                total[market],
                (((1,), (1,)), ((), ())),
                precision=lax.Precision.HIGHEST,
                preferred_element_type=F32,
            )
            row = summed[0:1, :] + outer[market : market + 1, :]
            for half in range(row.shape[1] // LANES):
                pieces.append(row[:, half * LANES : (half + 1) * LANES])
        sums_ref[...] = jnp.concatenate(pieces, axis=0)


def split_products(traits_hbm, level_ref, traits_out, traits_vmem, arrived):
    part_len = traits_vmem.shape[1]
    own = lax.axis_index("draw")
    copy = pltpu.make_async_copy(
        traits_hbm.at[:, pl.ds(pl.multiple_of(own * part_len, part_len), part_len)], traits_vmem, arrived
    )
    copy.start()
    copy.wait()
    blocks = part_len // BLOCK

    def step(block, carry):
        start = pl.multiple_of(block * BLOCK, BLOCK)
        rows = trait_rows(traits_vmem[:, pl.ds(start, BLOCK)], level_row(level_ref, own * blocks + block))
        traits_out[pl.ds(start, BLOCK), :] = jnp.concatenate(rows, axis=0).T.astype(BF16)
        return carry

    lax.fori_loop(0, blocks, step, 0, unroll=2)


def group_at(place, stages):
    own = lax.axis_index("draw")
    group = own
    for stride, factor in stages:
        digit = lax.rem(own // stride, factor)
        shift = place % factor
        place //= factor
        group = group + (lax.rem(digit - shift + factor, factor) - digit) * stride
    return group


def split_draws(count, scale_ref, *refs):
    draws_refs, right_out = refs[:count], refs[count]
    group = draws_refs[0].shape[2]
    index = 0
    for ref in draws_refs:
        for place in range(ref.shape[0]):
            right_out[:, index * group : (index + 1) * group] = stacked(taste_rows(ref[place], scale_ref[...]))
            index += 1


def fill(offset, traits_ref, right_ref, expo_ref):
    blocks, kept = expo_ref.shape[0] // BLOCK, expo_ref.shape[1]

    def step(block, carry):
        start = pl.multiple_of(block * BLOCK, BLOCK)
        left = traits_ref[pl.ds(start, BLOCK), :]

        def columns(begin):
            expo_ref[pl.ds(start, BLOCK), pl.ds(begin, 256)] = jnp.exp2(mm(left, right_ref[:, pl.ds(offset + begin, 256)]))

        if kept <= 2048:
            for begin in range(0, kept, 256):
                columns(begin)
        else:

            def inner(index, carry):
                columns(pl.multiple_of(index * 256, 256))
                return carry

            lax.fori_loop(0, kept // 256, inner, 0)
        return carry

    lax.fori_loop(0, blocks, step, 0, unroll=4)


def inverse_rows(inverse, pieces):
    for group, tile in enumerate(pieces):
        flipped = 1.0 / tile
        halves = tile.shape[0] // MARKETS
        for market in range(MARKETS):
            for half in range(halves):
                row = market * halves + half
                start = (group * halves + half) * LANES
                inverse[market, 0:1, start : start + LANES] = flipped[row : row + 1, :]


def over_columns(width, body, carry):
    tiles = width // LANES
    if tiles <= 16:
        for tile in range(tiles):
            carry = body(tile * LANES, carry)
        return carry
    return lax.fori_loop(0, tiles, lambda tile, kept: body(pl.multiple_of(tile * LANES, LANES), kept), carry)


def share_sum(expo_refs, rest_expo, inverse, market, start):
    total = jnp.zeros((BLOCK, LANES), F32)
    offset = 0
    for ref in expo_refs + (rest_expo,):
        first = 0 if ref is rest_expo else start

        def columns(begin, total, ref=ref, first=first, offset=offset):
            terms = ref[pl.ds(first, BLOCK), pl.ds(begin, LANES)]
            return total + terms * inverse[market, 0:1, pl.ds(offset + begin, LANES)]

        total = over_columns(ref.shape[1], columns, total)
        offset += ref.shape[1]
    return jnp.sum(total, axis=1, keepdims=True)


def rest_columns_of(rest_expo, traits_ref, rest_ref, start):
    left = traits_ref[pl.ds(start, BLOCK), :]
    for begin in range(0, rest_expo.shape[1], 256):
        rest_expo[:, begin : begin + 256] = jnp.exp2(mm(left, rest_ref[:, pl.ds(rest_ref.shape[1] - rest_expo.shape[1] + begin, 256)]))


def own_rows(ref, blocks):
    base = lax.axis_index("draw") * (blocks * HALVES)
    return jnp.concatenate(
        [ref[pl.ds(base + half, blocks, stride=HALVES), :] for half in range(HALVES)], axis=1
    )


def both_sums(market_scale, share_scale, stages, counts, market_ref, *refs):
    sums_refs, refs = refs[: counts[0]], refs[counts[0] :]
    (target_ref, outside_ref, traits_ref, right_ref), refs = refs[:4], refs[4:]
    expo_refs, refs = refs[: counts[1]], refs[counts[1] :]
    share_ref, next_ref, inverse, total, growth, rest_expo = refs
    blocks = expo_refs[0].shape[0] // BLOCK
    groups = next_ref.shape[0]
    own = lax.axis_index("draw")
    inverse_rows(inverse, [ref[place] for ref in sums_refs for place in range(ref.shape[0])])
    total[...] = jnp.zeros_like(total)
    wanted = jnp.exp(own_rows(target_ref, blocks)) / share_scale
    if blocks < LANES:
        wanted = jnp.concatenate([wanted, jnp.ones((LANES - blocks, BLOCK), F32)], axis=0)
    growth[...] = wanted.T
    share_ref[...] = jnp.ones_like(share_ref)
    lane = lax.broadcasted_iota(jnp.int32, (BLOCK, LANES), 1)

    def step(block, carry):
        start = pl.multiple_of(block * BLOCK, BLOCK)
        market = market_ref[own * blocks + block]
        rest_columns_of(rest_expo, traits_ref, right_ref, start)
        share = share_sum(expo_refs, rest_expo, inverse, market, start)
        here = lane == block
        factor = jnp.sum(jnp.where(here, growth[...], 0.0), axis=1, keepdims=True)
        share_ref[...] = jnp.where(here, share, share_ref[...])
        factor = jnp.broadcast_to(factor / share, (BLOCK, LANES))
        offset = 0
        for ref in expo_refs + (rest_expo,):
            first = 0 if ref is rest_expo else start

            def columns(begin, carry, ref=ref, first=first, offset=offset):
                terms = ref[pl.ds(first, BLOCK), pl.ds(begin, LANES)] * factor
                total[market, :, pl.ds(offset + begin, LANES)] += terms.reshape(BLOCK // 8, 8, LANES).sum(axis=0)
                return carry

            over_columns(ref.shape[1], columns, 0)
            offset += ref.shape[1]
        return carry

    lax.fori_loop(0, blocks, step, 0, unroll=2)
    halves = next_ref.shape[1] // MARKETS
    mine = jnp.where(lax.axis_index("prod") == 0, market_scale, 0.0)
    outer = mine * jnp.exp(outside_ref[...])
    for place in range(groups):
        rows = []
        for market in range(MARKETS):
            for half in range(halves):
                begin = (place * halves + half) * LANES
                row = jnp.sum(total[market, :, begin : begin + LANES], axis=0, keepdims=True)
                if place == 0:
                    row = row + outer[market : market + 1, half * LANES : (half + 1) * LANES]
                rows.append(row)
        next_ref[group_at(place, stages)] = jnp.concatenate(rows, axis=0)


def last_sums(share_scale, stages, counts, market_ref, *refs):
    sums_refs, refs = refs[: counts[0]], refs[counts[0] :]
    (target_ref, level_ref, traits_ref, right_ref), refs = refs[:4], refs[4:]
    expo_refs, refs = refs[: counts[1]], refs[counts[1] :]
    share_ref, out_level, out_residual, inverse, second, rest_expo = refs
    blocks = expo_refs[0].shape[0] // BLOCK
    own = lax.axis_index("draw")
    pieces = []
    for place in range(sums_refs[0].shape[0]):
        group = group_at(place, stages)
        tile = sums_refs[0][group]
        for ref in sums_refs[1:]:
            tile = tile + ref[group]
        pieces.append(tile)
    inverse_rows(inverse, pieces)
    second[...] = jnp.ones_like(second)
    lane = lax.broadcasted_iota(jnp.int32, (BLOCK, LANES), 1)

    def step(block, carry):
        start = pl.multiple_of(block * BLOCK, BLOCK)
        market = market_ref[own * blocks + block]
        rest_columns_of(rest_expo, traits_ref, right_ref, start)
        share = share_sum(expo_refs, rest_expo, inverse, market, start)
        second[...] = jnp.where(lane == block, share, second[...])
        return carry

    lax.fori_loop(0, blocks, step, 0, unroll=2)
    before = share_ref[...].T[:blocks]
    after = second[...].T[:blocks]
    residual = jnp.log(before) - jnp.log(after)
    level = own_rows(level_ref, blocks) + own_rows(target_ref, blocks) - jnp.log(after * share_scale)
    for half in range(HALVES):
        columns = slice(half * LANES, (half + 1) * LANES)
        out_residual[pl.ds(half, blocks, stride=HALVES), :] = residual[:, columns]
        out_level[pl.ds(half, blocks, stride=HALVES), :] = level[:, columns]


def digit_pairs(size, stride, factor, shift):
    pairs = []
    for index in range(size):
        digit = index // stride % factor
        pairs.append((index, index + ((digit + shift) % factor - digit) * stride))
    return pairs


def shifted(values, axis, stride, factor):
    size = lax.axis_size(axis)
    return [values] + [
        lax.ppermute(values, axis, digit_pairs(size, stride, factor, shift)) for shift in range(1, factor)
    ]


def collected(values, stages):
    parts = [values[None]]
    for stride, factor in stages:
        joined = parts[0] if len(parts) == 1 else jnp.concatenate(parts, axis=0)
        parts = shifted(joined, "draw", stride, factor)
    return parts


def total_of(parts):
    return functools.reduce(jnp.add, parts)


def body(product_traits, mean_utility, target, taste_scale, taste_draws, outside, block_market):
    k_count, prod_count = product_traits.shape
    group = taste_draws.shape[1]
    draw_devices = lax.axis_size("draw")
    prod_devices = lax.axis_size("prod")
    draws = group * draw_devices
    market_scale = float(prod_count * prod_devices // MARKETS)
    share_scale = market_scale / float(draws)
    part_len = prod_count // draw_devices
    depth = 3 * k_count + 16
    tile_rows = MARKETS * group // LANES
    cells = prod_count * group

    level_rows = mean_utility.reshape(-1, LANES)
    target_rows = target.reshape(-1, LANES)
    scale_row = taste_scale.reshape(1, k_count)

    stages = []
    stride = 1
    while stride < draw_devices:
        factor = 2 if stride == 1 else math.gcd(4, draw_devices // stride)
        stages.append((stride, factor))
        stride *= factor

    def grant(rest):
        return 4 * (draws * MARKETS * 16 + BLOCK * rest + 2**19)

    fixed = 2 * depth * draws + 2 * LANES * part_len
    eighths = max(
        count for count in range(1, 8) if fixed + draws // 8 * count * part_len * 4 + grant(draws - draws // 8 * count) < BUDGET
    )
    kept = draws // 8 * eighths
    rest = draws - kept
    bounds = [draws // 8 * (eighths * index // PIECES) for index in range(PIECES + 1)]
    held_params = pltpu.CompilerParams(vmem_limit_bytes=max(grant(rest), FLOOR))

    every_draw = collected(taste_draws, stages)

    step_len = min(STEP_BLOCKS * BLOCK, prod_count)
    whole = lambda shape: pl.BlockSpec(shape, lambda step, market: (0,) * len(shape))
    first = pl.pallas_call(
        functools.partial(first_sums, market_scale),
        grid_spec=pltpu.PrefetchScalarGridSpec(
            num_scalar_prefetch=1,
            grid=(prod_count // step_len,),
            in_specs=[
                pl.BlockSpec((k_count, step_len), lambda step, market: (0, step)),
                pl.BlockSpec((step_len // LANES, LANES), lambda step, market: (step, 0)),
                whole((1, k_count)),
                whole((k_count, group)),
                whole((MARKETS, group)),
            ],
            out_specs=whole((tile_rows, LANES)),
            scratch_shapes=[
                pltpu.VMEM((group, depth), BF16),
                pltpu.VMEM((MARKETS, group, LANES), F32),
            ],
        ),
        out_shape=jax.ShapeDtypeStruct((tile_rows, LANES), F32),
        compiler_params=params((k_count, step_len), (k_count, step_len), (MARKETS, group, LANES), (BLOCK, step_len), (2**20,)),
        cost_estimate=pl.CostEstimate(flops=2 * cells * 256, bytes_accessed=4 * k_count * prod_count, transcendentals=cells),
        name="first_sums",
    )(*[pltpu.with_memory_space_constraint(array, pltpu.HBM) for array in (block_market, product_traits, level_rows, scale_row, taste_draws, outside)])

    sums = collected(total_of(shifted(first, "prod", 1, prod_devices)), stages)

    hbm_traits = pltpu.with_memory_space_constraint(product_traits, pltpu.HBM)
    traits_split = pl.pallas_call(
        split_products,
        in_specs=[ANY, VMEM],
        out_specs=VMEM,
        out_shape=pltpu.VMEM((part_len, depth), BF16),
        scratch_shapes=[pltpu.VMEM((k_count, part_len), F32), pltpu.SemaphoreType.DMA],
        compiler_params=params((k_count, part_len), (prod_count,), (depth, part_len)),
        name="split_products",
    )(hbm_traits, level_rows)
    draws_split = pl.pallas_call(
        functools.partial(split_draws, len(every_draw)),
        in_specs=[VMEM] * (1 + len(every_draw)),
        out_specs=VMEM,
        out_shape=pltpu.VMEM((depth, draws), BF16),
        compiler_params=params((k_count, draws), (depth, draws)),
        name="split_draws",
    )(scale_row, *every_draw)
    traits_split, draws_split = [
        pltpu.with_memory_space_constraint(array, pltpu.VMEM) for array in (traits_split, draws_split)
    ]
    expo = []
    for begin, end in zip(bounds, bounds[1:]):
        piece = pl.pallas_call(
            functools.partial(fill, begin),
            in_specs=[VMEM, VMEM],
            out_specs=VMEM,
            out_shape=pltpu.VMEM((part_len, end - begin), F32),
            compiler_params=held_params,
            cost_estimate=pl.CostEstimate(
                flops=2 * part_len * (end - begin) * 256, bytes_accessed=2**20, transcendentals=part_len * (end - begin)
            ),
            name="fill",
        )(traits_split, draws_split)
        expo.append(pltpu.with_memory_space_constraint(piece, pltpu.VMEM))
    held = (traits_split, draws_split, *expo)

    share, partial = pl.pallas_call(
        functools.partial(both_sums, market_scale, share_scale, stages, (len(sums), len(expo))),
        in_specs=[SMEM] + [VMEM] * (len(sums) + 4 + len(expo)),
        out_specs=(VMEM, VMEM),
        out_shape=(
            jax.ShapeDtypeStruct((BLOCK, LANES), F32),
            jax.ShapeDtypeStruct((draw_devices, tile_rows, LANES), F32),
        ),
        scratch_shapes=[
            pltpu.VMEM((MARKETS, 8, draws), F32),
            pltpu.VMEM((MARKETS, 8, draws), F32),
            pltpu.VMEM((BLOCK, LANES), F32),
            pltpu.VMEM((BLOCK, rest), F32),
        ],
        compiler_params=held_params,
        cost_estimate=pl.CostEstimate(flops=4 * cells, bytes_accessed=2**20, transcendentals=0),
        name="both_sums",
    )(block_market, *sums, target_rows, outside, *held)

    parts = shifted(partial, "prod", 1, prod_devices)
    for stride, factor in stages:
        parts = shifted(total_of(parts), "draw", stride, factor)

    level, residual = pl.pallas_call(
        functools.partial(last_sums, share_scale, stages, (len(parts), len(expo))),
        in_specs=[SMEM] + [VMEM] * (len(parts) + 4 + len(expo) + 1),
        out_specs=(VMEM, VMEM),
        out_shape=(jax.ShapeDtypeStruct((part_len // LANES, LANES), F32),) * 2,
        scratch_shapes=[
            pltpu.VMEM((MARKETS, 8, draws), F32),
            pltpu.VMEM((BLOCK, LANES), F32),
            pltpu.VMEM((BLOCK, rest), F32),
        ],
        compiler_params=held_params,
        cost_estimate=pl.CostEstimate(flops=2 * cells, bytes_accessed=2**20, transcendentals=0),
        name="last_sums",
    )(block_market, *parts, target_rows, level_rows, *held, share)
    return level.reshape(-1), residual.reshape(-1)


def solution(mesh):
    placed = (
        P(None, "prod"),
        P("prod"),
        P("prod"),
        P(),
        P(None, "draw"),
        P(None, "draw"),
        P("prod"),
    )
    return jax.shard_map(
        body,
        mesh=mesh,
        in_specs=placed,
        out_specs=(P(("prod", "draw")), P(("prod", "draw"))),
        check_vma=False,
    )
```

time: 648 us -> 93.1 us (0.14)
  matrix products: 303 us -> 0 us
  waiting for transfers between devices: 141 us -> 12.3 us
  local copies, waits for them, and re-layouts: 119 us -> 7.08 us
  Pallas kernels: 0 us -> 50.9 us
  other arithmetic: 44.9 us -> 0.79 us
  starting transfers between devices: 0.08 us -> 20.9 us
  blocking collectives: 14 us -> 0 us
  between operations: 14.1 us -> 0.82 us
  loops' own time: 9.99 us -> 0 us
    dot_general x50 -> x0, matrix products: 303 us -> none  [the longest x16 185 us: exp_tile(): jnp.dot(taste_mix.T, columns, precision=lax.Precision.HIGHEST, preferred_...]
    psum x2 -> x0, waiting for transfers between devices: 141 us -> none  [body(): share_full = lax.psum(local_share, 'draw')]
    dynamic_slice x48 -> x0, local copies, waits for them, and re-layouts: 72.2 us -> none  [the longest x16 62.8 us: body(): lax.map(lambda tile_pair: share_tile(tile_pair[0], tile_pair[1], inverse)...]
    pallas_call x0 -> x8, Pallas kernels: none -> 50.9 us  [the longest x1 14.3 us: body(): pl.pallas_call(functools.partial(first_sums, market_scale), grid_spec=plt...]
    another operation x4 -> x0, local copies, waits for them, and re-layouts: 42 us -> none
    reduce_sum x2 -> x0, other arithmetic: 41.4 us -> none  [market_sums(): block_sums = expo_tile.reshape(draws_here, block_count, BLOCK).sum(axis=2)]
    ppermute x0 -> x18, starting transfers between devices: none -> 20.9 us  [shifted(): lax.ppermute(values, axis, digit_pairs(size, stride, factor, shift))]
    psum x2 -> x0, blocking collectives: 14 us -> none  [body(): denominator = lax.psum(local_sums, 'prod') + outside_term]
  transfers between devices with their start and end apart: 2 -> 18, of which waited for: 2 -> 8; matrix products, arithmetic and copies ran while one was open for 0% -> 0% of each run, Pallas kernels for 0% -> 14%
where the time goes in v1:
time: 93.1 us; the launch traced here: 92.8 us
  Pallas kernels  50.9 us (55%)
  starting transfers between devices  20.9 us (22%)
  waiting for transfers between devices  12.3 us (13%)
  local copies, waits for them, and re-layouts  7.08 us (8%)
    ppermute x18, starting transfers between devices, shifted(): lax.ppermute(values, axis, digit_pairs(size, stride, factor, shift))  20.9 us
    pallas_call x1, Pallas kernels, body(): pl.pallas_call(functools.partial(first_sums, market_scale), grid_spec=plt...  14.3 us
    pallas_call x1, Pallas kernels, body(): pl.pallas_call(functools.partial(both_sums, market_scale, share_scale, st...  13.8 us
    ppermute x18, waiting for transfers between devices, shifted(): lax.ppermute(values, axis, digit_pairs(size, stride, factor, shift))  12.3 us
    pallas_call x3, Pallas kernels, body(): pl.pallas_call(functools.partial(fill, begin), in_specs=[VMEM, VMEM], out...  10.1 us
    pallas_call x1, Pallas kernels, body(): pl.pallas_call(functools.partial(last_sums, share_scale, stages, (len(par...  9.45 us
    unnamed x26, local copies, waits for them, and re-layouts  7.08 us
    pallas_call x1, Pallas kernels, body(): pl.pallas_call(split_products, in_specs=[ANY, VMEM], out_specs=VMEM, out_...  3.08 us
  transfers between devices with their start and end apart: 18, of which 8 were waited for; matrix products, arithmetic and copies ran while one was open for 0% of the time, Pallas kernels for 14%

profile of v1, /device:TPU:0, one launch (start us, length us, event | category | flops | bytes accessed | tf_op | source)
XLA Modules:
  0.0 92.8 jit_solution(5371278305737172403)
XLA Ops:
  0.7 14.3 %first_sums.1 = f32[8,128]{1,0:T(8,128)S(1)} custom-call(s32[256]{0:T(256)} %market_ref.5, f32[32,65536]{1,0:T(8,128)} %traits_hbm.1, f32[512,128]{1,0:T(8,128)} %bitcast.8, f32[1,32]{1,0:T(1,128)} %bitcast.11, f32[32,256]{1,0:T(8,128)} %draws_ref.1, f32[4,256]{1,0:T(4,128)} %refs_5_.1), custom_call_target="tpu_custom_call" | custom-call | flops 8589934592 | bytes 8388608 | tf_op jit(solution)/shard_map/first_sums/pallas_call | solution.py:393
  15.0 2.4 %collective-permute-start.2 = (f32[8,128]{1,0:T(8,128)S(1)}, f32[8,128]{1,0:T(8,128)S(1)}, u32[]{:S(2)}, u32[]{:S(2)}) collective-permute-start(f32[8,128]{1,0:T(8,128)S(1)} %first_sums.1), channel_id=1, source_target_pairs={{0,24},{8,0},{16,8},{24,16},{1,25},{9,1},{17,9},{25,17},{2,26},{10... | collective-permute-start | bytes 12296 | tf_op jit(solution)/shard_map/ppermute | solution.py:337
  17.4 0.6 collective-permute-start.1
  18.2 1.5 %collective-permute-start.7 = (f32[1,32,256]{2,1,0:T(8,128)S(1)}, f32[1,32,256]{2,1,0:T(8,128)S(1)}, u32[]{:S(2)}, u32[]{:S(2)}) collective-permute-start(f32[1,32,256]{2,1,0:T(8,128)S(1)} %bitcast.15), channel_id=1, source_target_pairs={{0,1},{1,0},{2,3},{3,2},{4,5},{5,4},{6,7},{7,6},{8,9},{9,8},{10,11... | collective-permute-start | bytes 98312 | tf_op jit(solution)/shard_map/ppermute | solution.py:337
  19.7 3.1 %split_products.1.traits_ref.refs_6_ = bf16[8192,112]{1,0:T(8,128)(2,1)S(1)} custom-call(f32[32,65536]{1,0:T(8,128)} %traits_hbm.1, f32[512,128]{1,0:T(8,128)S(1)} %bitcast.10), custom_call_target="tpu_custom_call" | custom-call | tf_op jit(solution)/shard_map/split_products/pallas_call | solution.py:420
  22.9 0.6 collective-permute-start.3
  23.5 3.7 %collective-permute-start.10 = (f32[2,32,256]{2,1,0:T(8,128)S(1)}, f32[2,32,256]{2,1,0:T(8,128)S(1)}, u32[]{:S(2)}, u32[]{:S(2)}) collective-permute-start(f32[2,32,256]{2,1,0:T(8,128)S(1)} %pad_maximum_fusion.refs_0_), channel_id=1, source_target_pairs={{0,6},{1,7},{2,0},{3,1},{4,2},{5,3},{6,4},{7,5},{8,14},{9,15},{10,... | collective-permute-start | bytes 196616 | tf_op jit(solution)/shard_map/ppermute | solution.py:337
  27.1 1.0 %collective-permute-start.8 = (f32[2,32,256]{2,1,0:T(8,128)S(1)}, f32[2,32,256]{2,1,0:T(8,128)S(1)}, u32[]{:S(2)}, u32[]{:S(2)}) collective-permute-start(f32[2,32,256]{2,1,0:T(8,128)S(1)} %pad_maximum_fusion.refs_0_), channel_id=1, source_target_pairs={{0,2},{1,3},{2,4},{3,5},{4,6},{5,7},{6,0},{7,1},{8,10},{9,11},{10,... | collective-permute-start | bytes 196616 | tf_op jit(solution)/shard_map/ppermute | solution.py:337
  28.2 2.9 %collective-permute-start.6 = (f32[2,8,128]{2,1,0:T(8,128)S(1)}, f32[2,8,128]{2,1,0:T(8,128)S(1)}, u32[]{:S(2)}, u32[]{:S(2)}) collective-permute-start(f32[2,8,128]{2,1,0:T(8,128)S(1)} %pad_maximum_fusion.1.refs_0_), channel_id=1, source_target_pairs={{0,6},{1,7},{2,0},{3,1},{4,2},{5,3},{6,4},{7,5},{8,14},{9,15},{10,... | collective-permute-start | bytes 24584 | tf_op jit(solution)/shard_map/ppermute | solution.py:337
  31.0 1.1 %collective-permute-start.5 = (f32[2,8,128]{2,1,0:T(8,128)S(1)}, f32[2,8,128]{2,1,0:T(8,128)S(1)}, u32[]{:S(2)}, u32[]{:S(2)}) collective-permute-start(f32[2,8,128]{2,1,0:T(8,128)S(1)} %pad_maximum_fusion.1.refs_0_), channel_id=1, source_target_pairs={{0,4},{1,5},{2,6},{3,7},{4,0},{5,1},{6,2},{7,3},{8,12},{9,13},{10,... | collective-permute-start | bytes 24584 | tf_op jit(solution)/shard_map/ppermute | solution.py:337
  32.2 2.5 %collective-permute-done.9.refs_2_ = f32[2,32,256]{2,1,0:T(8,128)S(1)} collective-permute-done((f32[2,32,256]{2,1,0:T(8,128)S(1)}, f32[2,32,256]{2,1,0:T(8,128)S(1)}, u32[]{:S(2)}, u32[]{:S(2)}) %collective-permute-start.9) | collective-permute-done | bytes 65568 | tf_op jit(solution)/shard_map/ppermute | solution.py:337
  34.8 3.4 %fill.5.refs_10_ = f32[8192,512]{1,0:T(8,128)S(1)} custom-call(bf16[8192,112]{1,0:T(8,128)(2,1)S(1)} %split_products.1.traits_ref.refs_6_, bf16[112,2048]{1,0:T(8,128)(2,1)S(1)} %split_draws.1.right_ref.refs_7_), custom_call_target="tpu_custom_call" | custom-call | flops 2147483648 | bytes 1048576 | tf_op jit(solution)/shard_map/fill/pallas_call | solution.py:442
  38.2 3.4 %fill.4.refs_9_ = f32[8192,512]{1,0:T(8,128)S(1)} custom-call(bf16[8192,112]{1,0:T(8,128)(2,1)S(1)} %split_products.1.traits_ref.refs_6_, bf16[112,2048]{1,0:T(8,128)(2,1)S(1)} %split_draws.1.right_ref.refs_7_), custom_call_target="tpu_custom_call" | custom-call | flops 2147483648 | bytes 1048576 | tf_op jit(solution)/shard_map/fill/pallas_call | solution.py:442
  41.6 3.4 %fill.3.refs_8_ = f32[8192,512]{1,0:T(8,128)S(1)} custom-call(bf16[8192,112]{1,0:T(8,128)(2,1)S(1)} %split_products.1.traits_ref.refs_6_, bf16[112,2048]{1,0:T(8,128)(2,1)S(1)} %split_draws.1.right_ref.refs_7_), custom_call_target="tpu_custom_call" | custom-call | flops 2147483648 | bytes 1048576 | tf_op jit(solution)/shard_map/fill/pallas_call | solution.py:442
  45.0 0.6 copy-done.10
  45.7 13.8 %both_sums.1 = (f32[256,128]{1,0:T(8,128)}, f32[8,8,128]{2,1,0:T(8,128)}) custom-call(s32[256]{0:T(256)} %market_ref.5, f32[2,8,128]{2,1,0:T(8,128)} %copy-done.9, f32[2,8,128]{2,1,0:T(8,128)} %copy-done.12, f32[2,8,128]{2,1,0:T(8,128)} %copy-done.11, f32[2,8,128]{2,1,0:T(8,128)} %copy-done.10, f32[512,128]{1,0:T(8,128)} %bitcast.13, f32[4,256]{1,0:T(4,128)} %refs_5_.1, ...), custom_call_target="tpu_custom_call" | custom-call | flops 67108864 | bytes 1048576 | tf_op jit(solution)/shard_map/both_sums/pallas_call | solution.py:456
  59.6 1.6 %collective-permute-start.12 = (f32[8,8,128]{2,1,0:T(8,128)}, f32[8,8,128]{2,1,0:T(8,128)S(1)}, u32[]{:S(2)}, u32[]{:S(2)}) collective-permute-start(f32[8,8,128]{2,1,0:T(8,128)} %get-tuple-element.6), channel_id=1, source_target_pairs={{0,16},{8,24},{16,0},{24,8},{1,17},{9,25},{17,1},{25,9},{2,18},{10... | collective-permute-start | bytes 98312 | tf_op jit(solution)/shard_map/ppermute | solution.py:337
  61.2 0.3 collective-permute-done.13
  61.5 2.4 %collective-permute-done.12 = f32[8,8,128]{2,1,0:T(8,128)S(1)} collective-permute-done((f32[8,8,128]{2,1,0:T(8,128)}, f32[8,8,128]{2,1,0:T(8,128)S(1)}, u32[]{:S(2)}, u32[]{:S(2)}) %collective-permute-start.12) | collective-permute-done | bytes 32800 | tf_op jit(solution)/shard_map/ppermute | solution.py:337
  63.9 0.8 collective-permute-done.11
  64.8 0.8 add_add_fusion
  65.5 1.6 %collective-permute-start.14 = (f32[8,8,128]{2,1,0:T(8,128)S(1)}, f32[8,8,128]{2,1,0:T(8,128)S(1)}, u32[]{:S(2)}, u32[]{:S(2)}) collective-permute-start(f32[8,8,128]{2,1,0:T(8,128)S(1)} %add_add_fusion), channel_id=1, source_target_pairs={{0,1},{1,0},{2,3},{3,2},{4,5},{5,4},{6,7},{7,6},{8,9},{9,8},{10,11... | collective-permute-start | bytes 98312 | tf_op jit(solution)/shard_map/ppermute | solution.py:337
  67.1 2.4 %collective-permute-done.14 = f32[8,8,128]{2,1,0:T(8,128)S(1)} collective-permute-done((f32[8,8,128]{2,1,0:T(8,128)S(1)}, f32[8,8,128]{2,1,0:T(8,128)S(1)}, u32[]{:S(2)}, u32[]{:S(2)}) %collective-permute-start.14) | collective-permute-done | bytes 32800 | tf_op jit(solution)/shard_map/ppermute | solution.py:337
  69.5 1.0 %collective-permute-start.17 = (f32[8,8,128]{2,1,0:T(8,128)S(1)}, f32[8,8,128]{2,1,0:T(8,128)S(1)}, u32[]{:S(2)}, u32[]{:S(2)}) collective-permute-start(f32[8,8,128]{2,1,0:T(8,128)S(1)} %add.27.refs_0_), channel_id=1, source_target_pairs={{0,6},{1,7},{2,0},{3,1},{4,2},{5,3},{6,4},{7,5},{8,14},{9,15},{10,... | collective-permute-start | bytes 98312 | tf_op jit(solution)/shard_map/ppermute | solution.py:337
  70.5 0.7 collective-permute-start.16
  71.2 1.9 %collective-permute-start.15 = (f32[8,8,128]{2,1,0:T(8,128)S(1)}, f32[8,8,128]{2,1,0:T(8,128)S(1)}, u32[]{:S(2)}, u32[]{:S(2)}) collective-permute-start(f32[8,8,128]{2,1,0:T(8,128)S(1)} %add.27.refs_0_), channel_id=1, source_target_pairs={{0,2},{1,3},{2,4},{3,5},{4,6},{5,7},{6,0},{7,1},{8,10},{9,11},{10,... | collective-permute-start | bytes 98312 | tf_op jit(solution)/shard_map/ppermute | solution.py:337
  73.2 0.6 collective-permute-done.17.refs_3_
  73.8 1.6 %collective-permute-done.16.refs_2_ = f32[8,8,128]{2,1,0:T(8,128)S(1)} collective-permute-done((f32[8,8,128]{2,1,0:T(8,128)S(1)}, f32[8,8,128]{2,1,0:T(8,128)S(1)}, u32[]{:S(2)}, u32[]{:S(2)}) %collective-permute-start.16) | collective-permute-done | bytes 32800 | tf_op jit(solution)/shard_map/ppermute | solution.py:337
  75.4 1.6 %collective-permute-done.15.refs_1_ = f32[8,8,128]{2,1,0:T(8,128)S(1)} collective-permute-done((f32[8,8,128]{2,1,0:T(8,128)S(1)}, f32[8,8,128]{2,1,0:T(8,128)S(1)}, u32[]{:S(2)}, u32[]{:S(2)}) %collective-permute-start.15) | collective-permute-done | bytes 32800 | tf_op jit(solution)/shard_map/ppermute | solution.py:337
  76.9 0.6 copy-done.8
  77.5 5.8 %copy-done.1 = f32[8192,512]{1,0:T(8,128)S(1)} copy-done((f32[8192,512]{1,0:T(8,128)S(1)}, f32[8192,512]{1,0:T(8,128)}, u32[]{:S(2)}) %copy-start.1) | copy-done | bytes 16777240
  83.3 9.4 %last_sums.1 = (f32[64,128]{1,0:T(8,128)}, f32[64,128]{1,0:T(8,128)}) custom-call(s32[256]{0:T(256)} %market_ref.5, f32[8,8,128]{2,1,0:T(8,128)} %copy-done.4, f32[8,8,128]{2,1,0:T(8,128)} %copy-done.8, f32[8,8,128]{2,1,0:T(8,128)} %copy-done.7, f32[8,8,128]{2,1,0:T(8,128)} %copy-done.6, f32[512,128]{1,0:T(8,128)} %bitcast.14, f32[512,128]{1,0:T(8,128)} %bitcast.9, ...), custom_call_target="tpu_custom_call" | custom-call | flops 33554432 | bytes 1048576 | tf_op jit(solution)/shard_map/last_sums/pallas_call | solution.py:479
  (43 shorter events, 0.5 us)
Async XLA Ops:
  0.6 17.6 %copy-start.5 = (f32[32,256]{1,0:T(8,128)S(1)}, f32[32,256]{1,0:T(8,128)}, u32[]{:S(2)}) copy-start(f32[32,256]{1,0:T(8,128)} %draws_ref.1) | copy-start | bytes 98308
  0.6 19.1 %copy-start.2 = (f32[65536]{0:T(1024)S(1)}, f32[65536]{0:T(1024)}, u32[]{:S(2)}) copy-start(f32[65536]{0:T(1024)} %param.8) | copy-start | bytes 786436
  0.7 34.0 %copy-start.3 = (f32[32]{0:T(128)S(1)}, f32[32]{0:T(128)}, u32[]{:S(2)}) copy-start(f32[32]{0:T(128)} %param.10) | copy-start | bytes 388
  15.0 7.8 %collective-permute-start.2 = (f32[8,128]{1,0:T(8,128)S(1)}, f32[8,128]{1,0:T(8,128)S(1)}, u32[]{:S(2)}, u32[]{:S(2)}) collective-permute-start(f32[8,128]{1,0:T(8,128)S(1)} %first_sums.1), channel_id=1, source_target_pairs={{0,24},{8,0},{16,8},{24,16},{1,25},{9,1},{17,9},{25,17},{2,26},{10... | collective-permute-start | bytes 12296 | tf_op jit(solution)/shard_map/ppermute | solution.py:337
  17.4 5.4 %collective-permute-start.1 = (f32[8,128]{1,0:T(8,128)S(1)}, f32[8,128]{1,0:T(8,128)S(1)}, u32[]{:S(2)}, u32[]{:S(2)}) collective-permute-start(f32[8,128]{1,0:T(8,128)S(1)} %first_sums.1), channel_id=1, source_target_pairs={{0,16},{8,24},{16,0},{24,8},{1,17},{9,25},{17,1},{25,9},{2,18},{10... | collective-permute-start | bytes 12296 | tf_op jit(solution)/shard_map/ppermute | solution.py:337
  18.1 4.8 %collective-permute-start = (f32[8,128]{1,0:T(8,128)S(1)}, f32[8,128]{1,0:T(8,128)S(1)}, u32[]{:S(2)}, u32[]{:S(2)}) collective-permute-start(f32[8,128]{1,0:T(8,128)S(1)} %first_sums.1), channel_id=1, source_target_pairs={{0,8},{8,16},{16,24},{24,0},{1,9},{9,17},{17,25},{25,1},{2,10},{10... | collective-permute-start | bytes 12296 | tf_op jit(solution)/shard_map/ppermute | solution.py:337
  18.2 5.2 %collective-permute-start.7 = (f32[1,32,256]{2,1,0:T(8,128)S(1)}, f32[1,32,256]{2,1,0:T(8,128)S(1)}, u32[]{:S(2)}, u32[]{:S(2)}) collective-permute-start(f32[1,32,256]{2,1,0:T(8,128)S(1)} %bitcast.15), channel_id=1, source_target_pairs={{0,1},{1,0},{2,3},{3,2},{4,5},{5,4},{6,7},{7,6},{8,9},{9,8},{10,11... | collective-permute-start | bytes 98312 | tf_op jit(solution)/shard_map/ppermute | solution.py:337
  22.9 5.3 %collective-permute-start.3 = (f32[1,8,128]{2,1,0:T(8,128)S(1)}, f32[1,8,128]{2,1,0:T(8,128)S(1)}, u32[]{:S(2)}, u32[]{:S(2)}) collective-permute-start(f32[1,8,128]{2,1,0:T(8,128)S(1)} %add_bitcast_fusion), channel_id=1, source_target_pairs={{0,1},{1,0},{2,3},{3,2},{4,5},{5,4},{6,7},{7,6},{8,9},{9,8},{10,11... | collective-permute-start | bytes 12296 | tf_op jit(solution)/shard_map/ppermute | solution.py:337
  23.5 8.7 %collective-permute-start.10 = (f32[2,32,256]{2,1,0:T(8,128)S(1)}, f32[2,32,256]{2,1,0:T(8,128)S(1)}, u32[]{:S(2)}, u32[]{:S(2)}) collective-permute-start(f32[2,32,256]{2,1,0:T(8,128)S(1)} %pad_maximum_fusion.refs_0_), channel_id=1, source_target_pairs={{0,6},{1,7},{2,0},{3,1},{4,2},{5,3},{6,4},{7,5},{8,14},{9,15},{10,... | collective-permute-start | bytes 196616 | tf_op jit(solution)/shard_map/ppermute | solution.py:337
  27.1 7.5 %collective-permute-start.9 = (f32[2,32,256]{2,1,0:T(8,128)S(1)}, f32[2,32,256]{2,1,0:T(8,128)S(1)}, u32[]{:S(2)}, u32[]{:S(2)}) collective-permute-start(f32[2,32,256]{2,1,0:T(8,128)S(1)} %pad_maximum_fusion.refs_0_), channel_id=1, source_target_pairs={{0,4},{1,5},{2,6},{3,7},{4,0},{5,1},{6,2},{7,3},{8,12},{9,13},{10,... | collective-permute-start | bytes 196616 | tf_op jit(solution)/shard_map/ppermute | solution.py:337
  27.1 7.5 %collective-permute-start.8 = (f32[2,32,256]{2,1,0:T(8,128)S(1)}, f32[2,32,256]{2,1,0:T(8,128)S(1)}, u32[]{:S(2)}, u32[]{:S(2)}) collective-permute-start(f32[2,32,256]{2,1,0:T(8,128)S(1)} %pad_maximum_fusion.refs_0_), channel_id=1, source_target_pairs={{0,2},{1,3},{2,4},{3,5},{4,6},{5,7},{6,0},{7,1},{8,10},{9,11},{10,... | collective-permute-start | bytes 196616 | tf_op jit(solution)/shard_map/ppermute | solution.py:337
  28.2 13.4 %copy-start.9 = (f32[2,8,128]{2,1,0:T(8,128)}, f32[2,8,128]{2,1,0:T(8,128)S(1)}, u32[]{:S(2)}) copy-start(f32[2,8,128]{2,1,0:T(8,128)S(1)} %pad_maximum_fusion.1.refs_0_) | copy-start | bytes 24580
  28.2 16.8 %collective-permute-start.6 = (f32[2,8,128]{2,1,0:T(8,128)S(1)}, f32[2,8,128]{2,1,0:T(8,128)S(1)}, u32[]{:S(2)}, u32[]{:S(2)}) collective-permute-start(f32[2,8,128]{2,1,0:T(8,128)S(1)} %pad_maximum_fusion.1.refs_0_), channel_id=1, source_target_pairs={{0,6},{1,7},{2,0},{3,1},{4,2},{5,3},{6,4},{7,5},{8,14},{9,15},{10,... | collective-permute-start | bytes 24584 | tf_op jit(solution)/shard_map/ppermute | solution.py:337
  31.0 14.0 %collective-permute-start.5 = (f32[2,8,128]{2,1,0:T(8,128)S(1)}, f32[2,8,128]{2,1,0:T(8,128)S(1)}, u32[]{:S(2)}, u32[]{:S(2)}) collective-permute-start(f32[2,8,128]{2,1,0:T(8,128)S(1)} %pad_maximum_fusion.1.refs_0_), channel_id=1, source_target_pairs={{0,4},{1,5},{2,6},{3,7},{4,0},{5,1},{6,2},{7,3},{8,12},{9,13},{10,... | collective-permute-start | bytes 24584 | tf_op jit(solution)/shard_map/ppermute | solution.py:337
  32.1 12.9 %collective-permute-start.4 = (f32[2,8,128]{2,1,0:T(8,128)S(1)}, f32[2,8,128]{2,1,0:T(8,128)S(1)}, u32[]{:S(2)}, u32[]{:S(2)}) collective-permute-start(f32[2,8,128]{2,1,0:T(8,128)S(1)} %pad_maximum_fusion.1.refs_0_), channel_id=1, source_target_pairs={{0,2},{1,3},{2,4},{3,5},{4,6},{5,7},{6,0},{7,1},{8,10},{9,11},{10,... | collective-permute-start | bytes 24584 | tf_op jit(solution)/shard_map/ppermute | solution.py:337
  45.0 14.6 %copy-start = (f32[8192,512]{1,0:T(8,128)}, f32[8192,512]{1,0:T(8,128)S(1)}, u32[]{:S(2)}) copy-start(f32[8192,512]{1,0:T(8,128)S(1)} %fill.3.refs_8_) | copy-start | bytes 50331652
  45.0 0.6 copy-start.10
  45.0 0.7 copy-start.11
  45.0 0.7 copy-start.12
  59.6 1.9 %collective-permute-start.13 = (f32[8,8,128]{2,1,0:T(8,128)}, f32[8,8,128]{2,1,0:T(8,128)S(1)}, u32[]{:S(2)}, u32[]{:S(2)}) collective-permute-start(f32[8,8,128]{2,1,0:T(8,128)} %get-tuple-element.6), channel_id=1, source_target_pairs={{0,24},{8,0},{16,8},{24,16},{1,25},{9,1},{17,9},{25,17},{2,26},{10... | collective-permute-start | bytes 98312 | tf_op jit(solution)/shard_map/ppermute | solution.py:337
  59.6 4.4 %collective-permute-start.12 = (f32[8,8,128]{2,1,0:T(8,128)}, f32[8,8,128]{2,1,0:T(8,128)S(1)}, u32[]{:S(2)}, u32[]{:S(2)}) collective-permute-start(f32[8,8,128]{2,1,0:T(8,128)} %get-tuple-element.6), channel_id=1, source_target_pairs={{0,16},{8,24},{16,0},{24,8},{1,17},{9,25},{17,1},{25,9},{2,18},{10... | collective-permute-start | bytes 98312 | tf_op jit(solution)/shard_map/ppermute | solution.py:337
  61.2 3.6 %collective-permute-start.11 = (f32[8,8,128]{2,1,0:T(8,128)}, f32[8,8,128]{2,1,0:T(8,128)S(1)}, u32[]{:S(2)}, u32[]{:S(2)}) collective-permute-start(f32[8,8,128]{2,1,0:T(8,128)} %get-tuple-element.6), channel_id=1, source_target_pairs={{0,8},{8,16},{16,24},{24,0},{1,9},{9,17},{17,25},{25,1},{2,10},{10... | collective-permute-start | bytes 98312 | tf_op jit(solution)/shard_map/ppermute | solution.py:337
  65.5 4.0 %collective-permute-start.14 = (f32[8,8,128]{2,1,0:T(8,128)S(1)}, f32[8,8,128]{2,1,0:T(8,128)S(1)}, u32[]{:S(2)}, u32[]{:S(2)}) collective-permute-start(f32[8,8,128]{2,1,0:T(8,128)S(1)} %add_add_fusion), channel_id=1, source_target_pairs={{0,1},{1,0},{2,3},{3,2},{4,5},{5,4},{6,7},{7,6},{8,9},{9,8},{10,11... | collective-permute-start | bytes 98312 | tf_op jit(solution)/shard_map/ppermute | solution.py:337
  69.5 7.4 %copy-start.4 = (f32[8,8,128]{2,1,0:T(8,128)}, f32[8,8,128]{2,1,0:T(8,128)S(1)}, u32[]{:S(2)}) copy-start(f32[8,8,128]{2,1,0:T(8,128)S(1)} %add.27.refs_0_) | copy-start | bytes 98308
  69.5 4.3 %collective-permute-start.17 = (f32[8,8,128]{2,1,0:T(8,128)S(1)}, f32[8,8,128]{2,1,0:T(8,128)S(1)}, u32[]{:S(2)}, u32[]{:S(2)}) collective-permute-start(f32[8,8,128]{2,1,0:T(8,128)S(1)} %add.27.refs_0_), channel_id=1, source_target_pairs={{0,6},{1,7},{2,0},{3,1},{4,2},{5,3},{6,4},{7,5},{8,14},{9,15},{10,... | collective-permute-start | bytes 98312 | tf_op jit(solution)/shard_map/ppermute | solution.py:337
  70.5 4.8 %collective-permute-start.16 = (f32[8,8,128]{2,1,0:T(8,128)S(1)}, f32[8,8,128]{2,1,0:T(8,128)S(1)}, u32[]{:S(2)}, u32[]{:S(2)}) collective-permute-start(f32[8,8,128]{2,1,0:T(8,128)S(1)} %add.27.refs_0_), channel_id=1, source_target_pairs={{0,4},{1,5},{2,6},{3,7},{4,0},{5,1},{6,2},{7,3},{8,12},{9,13},{10,... | collective-permute-start | bytes 98312 | tf_op jit(solution)/shard_map/ppermute | solution.py:337
  71.2 5.7 %collective-permute-start.15 = (f32[8,8,128]{2,1,0:T(8,128)S(1)}, f32[8,8,128]{2,1,0:T(8,128)S(1)}, u32[]{:S(2)}, u32[]{:S(2)}) collective-permute-start(f32[8,8,128]{2,1,0:T(8,128)S(1)} %add.27.refs_0_), channel_id=1, source_target_pairs={{0,2},{1,3},{2,4},{3,5},{4,6},{5,7},{6,0},{7,1},{8,10},{9,11},{10,... | collective-permute-start | bytes 98312 | tf_op jit(solution)/shard_map/ppermute | solution.py:337
  73.8 3.1 %copy-start.6 = (f32[8,8,128]{2,1,0:T(8,128)}, f32[8,8,128]{2,1,0:T(8,128)S(1)}, u32[]{:S(2)}) copy-start(f32[8,8,128]{2,1,0:T(8,128)S(1)} %collective-permute-done.17.refs_3_) | copy-start | bytes 98308
  75.4 1.6 %copy-start.7 = (f32[8,8,128]{2,1,0:T(8,128)}, f32[8,8,128]{2,1,0:T(8,128)S(1)}, u32[]{:S(2)}) copy-start(f32[8,8,128]{2,1,0:T(8,128)S(1)} %collective-permute-done.16.refs_2_) | copy-start | bytes 98308
  76.9 0.6 copy-start.8
  77.5 5.8 %copy-start.1 = (f32[8192,512]{1,0:T(8,128)S(1)}, f32[8192,512]{1,0:T(8,128)}, u32[]{:S(2)}) copy-start(f32[8192,512]{1,0:T(8,128)} %copy-done) | copy-start | bytes 50331652

commit v2 on v1

--- a/solution.py
+++ b/solution.py
@@ -14,7 +14,7 @@
 HALVES = BLOCK // LANES
 LOG2E = math.log2(math.e)
 BUDGET = 58 * 2**20
-FLOOR = 8 * 2**20
+FLOOR = 10 * 2**20
 PIECES = 3
 STEP_BLOCKS = 32
 F32 = jnp.float32
@@ -77,7 +77,7 @@
     return lax.dot_general(left, right, (((1,), (0,)), ((), ())), preferred_element_type=F32)
 
 
-def first_sums(market_scale, market_ref, traits_ref, level_ref, scale_ref, draws_ref, outside_ref, sums_ref, left, total):
+def first_sums(market_scale, begin, market_ref, traits_ref, level_ref, scale_ref, draws_ref, before_ref, sums_ref, left, total):
     step = pl.program_id(0)
 
     @pl.when(step == 0)
@@ -87,7 +87,7 @@
         total[...] = jnp.zeros_like(total)
 
     for local in range(traits_ref.shape[1] // BLOCK):
-        block = step * (traits_ref.shape[1] // BLOCK) + local
+        block = (begin + step) * (traits_ref.shape[1] // BLOCK) + local
         right = stacked(
             trait_rows(traits_ref[:, local * BLOCK : (local + 1) * BLOCK], level_row(level_ref, local))
         )
@@ -100,8 +100,9 @@
 
     @pl.when(step == pl.num_programs(0) - 1)
     def _():
-        own = jnp.where(lax.axis_index("prod") == 0, market_scale, 0.0)
-        outer = own * jnp.exp(outside_ref[...])
+        if begin == 0:
+            own = jnp.where(lax.axis_index("prod") == 0, market_scale, 0.0)
+            outer = own * jnp.exp(before_ref[...])
         ones = jnp.ones((8, LANES), F32)
         pieces = []
         for market in range(MARKETS):
@@ -112,10 +113,13 @@
                 precision=lax.Precision.HIGHEST,
                 preferred_element_type=F32,
             )
-            row = summed[0:1, :] + outer[market : market + 1, :]
+            row = summed[0:1, :]
+            if begin == 0:
+                row = row + outer[market : market + 1, :]
             for half in range(row.shape[1] // LANES):
                 pieces.append(row[:, half * LANES : (half + 1) * LANES])
-        sums_ref[...] = jnp.concatenate(pieces, axis=0)
+        tile = jnp.concatenate(pieces, axis=0)
+        sums_ref[...] = tile if begin == 0 else tile + before_ref[...]
 
 
 def split_products(traits_hbm, level_ref, traits_out, traits_vmem, arrived):
@@ -148,14 +152,11 @@
     return group
 
 
-def split_draws(count, scale_ref, *refs):
-    draws_refs, right_out = refs[:count], refs[count]
-    group = draws_refs[0].shape[2]
-    index = 0
-    for ref in draws_refs:
-        for place in range(ref.shape[0]):
-            right_out[:, index * group : (index + 1) * group] = stacked(taste_rows(ref[place], scale_ref[...]))
-            index += 1
+def split_draws(stages, scale_ref, draws_ref, right_out):
+    group = draws_ref.shape[2]
+    for place in range(draws_ref.shape[0]):
+        rows = taste_rows(draws_ref[group_at(place, stages)], scale_ref[...])
+        right_out[:, place * group : (place + 1) * group] = stacked(rows)
 
 
 def fill(offset, traits_ref, right_ref, expo_ref):
@@ -191,7 +192,7 @@
             for half in range(halves):
                 row = market * halves + half
                 start = (group * halves + half) * LANES
-                inverse[market, 0:1, start : start + LANES] = flipped[row : row + 1, :]
+                inverse[market, :, start : start + LANES] = jnp.broadcast_to(flipped[row : row + 1, :], (8, LANES))
 
 
 def over_columns(width, body, carry):
@@ -204,18 +205,18 @@
 
 
 def share_sum(expo_refs, rest_expo, inverse, market, start):
-    total = jnp.zeros((BLOCK, LANES), F32)
+    total = jnp.zeros((BLOCK // 8, 8, LANES), F32)
     offset = 0
     for ref in expo_refs + (rest_expo,):
         first = 0 if ref is rest_expo else start
 
         def columns(begin, total, ref=ref, first=first, offset=offset):
-            terms = ref[pl.ds(first, BLOCK), pl.ds(begin, LANES)]
-            return total + terms * inverse[market, 0:1, pl.ds(offset + begin, LANES)]
+            terms = ref[pl.ds(first, BLOCK), pl.ds(begin, LANES)].reshape(BLOCK // 8, 8, LANES)
+            return total + terms * inverse[market, :, pl.ds(offset + begin, LANES)]
 
         total = over_columns(ref.shape[1], columns, total)
         offset += ref.shape[1]
-    return jnp.sum(total, axis=1, keepdims=True)
+    return jnp.sum(total.reshape(BLOCK, LANES), axis=1, keepdims=True)
 
 
 def rest_columns_of(rest_expo, traits_ref, rest_ref, start):
@@ -270,7 +271,7 @@
             offset += ref.shape[1]
         return carry
 
-    lax.fori_loop(0, blocks, step, 0, unroll=2)
+    lax.fori_loop(0, blocks, step, 0, unroll=4)
     halves = next_ref.shape[1] // MARKETS
     mine = jnp.where(lax.axis_index("prod") == 0, market_scale, 0.0)
     outer = mine * jnp.exp(outside_ref[...])
@@ -312,7 +313,7 @@
         second[...] = jnp.where(lane == block, share, second[...])
         return carry
 
-    lax.fori_loop(0, blocks, step, 0, unroll=2)
+    lax.fori_loop(0, blocks, step, 0, unroll=4)
     before = share_ref[...].T[:blocks]
     after = second[...].T[:blocks]
     residual = jnp.log(before) - jnp.log(after)
@@ -338,12 +339,15 @@
     ]
 
 
-def collected(values, stages):
-    parts = [values[None]]
+def collected(parts, stages):
     for stride, factor in stages:
         joined = parts[0] if len(parts) == 1 else jnp.concatenate(parts, axis=0)
         parts = shifted(joined, "draw", stride, factor)
     return parts
+
+
+def near(*arrays):
+    return [pltpu.with_memory_space_constraint(array, pltpu.VMEM) for array in arrays]
 
 
 def total_of(parts):
@@ -386,35 +390,47 @@
     bounds = [draws // 8 * (eighths * index // PIECES) for index in range(PIECES + 1)]
     held_params = pltpu.CompilerParams(vmem_limit_bytes=max(grant(rest), FLOOR))
 
-    every_draw = collected(taste_draws, stages)
-
-    step_len = min(STEP_BLOCKS * BLOCK, prod_count)
+    step_len = min(STEP_BLOCKS * BLOCK, prod_count // 2)
+    steps = prod_count // step_len
     whole = lambda shape: pl.BlockSpec(shape, lambda step, market: (0,) * len(shape))
-    first = pl.pallas_call(
-        functools.partial(first_sums, market_scale),
-        grid_spec=pltpu.PrefetchScalarGridSpec(
-            num_scalar_prefetch=1,
-            grid=(prod_count // step_len,),
-            in_specs=[
-                pl.BlockSpec((k_count, step_len), lambda step, market: (0, step)),
-                pl.BlockSpec((step_len // LANES, LANES), lambda step, market: (step, 0)),
-                whole((1, k_count)),
-                whole((k_count, group)),
-                whole((MARKETS, group)),
-            ],
-            out_specs=whole((tile_rows, LANES)),
-            scratch_shapes=[
-                pltpu.VMEM((group, depth), BF16),
-                pltpu.VMEM((MARKETS, group, LANES), F32),
-            ],
-        ),
-        out_shape=jax.ShapeDtypeStruct((tile_rows, LANES), F32),
-        compiler_params=params((k_count, step_len), (k_count, step_len), (MARKETS, group, LANES), (BLOCK, step_len), (2**20,)),
-        cost_estimate=pl.CostEstimate(flops=2 * cells * 256, bytes_accessed=4 * k_count * prod_count, transcendentals=cells),
-        name="first_sums",
-    )(*[pltpu.with_memory_space_constraint(array, pltpu.HBM) for array in (block_market, product_traits, level_rows, scale_row, taste_draws, outside)])
-
-    sums = collected(total_of(shifted(first, "prod", 1, prod_devices)), stages)
+
+    def first(begin, count, market, before):
+        arrays = (market, product_traits, level_rows, scale_row, taste_draws, before)
+        return pl.pallas_call(
+            functools.partial(first_sums, market_scale, begin),
+            grid_spec=pltpu.PrefetchScalarGridSpec(
+                num_scalar_prefetch=1,
+                grid=(count,),
+                in_specs=[
+                    pl.BlockSpec((k_count, step_len), lambda step, market: (0, step + begin)),
+                    pl.BlockSpec((step_len // LANES, LANES), lambda step, market: (step + begin, 0)),
+                    whole((1, k_count)),
+                    whole((k_count, group)),
+                    whole(before.shape),
+                ],
+                out_specs=whole((tile_rows, LANES)),
+                scratch_shapes=[
+                    pltpu.VMEM((group, depth), BF16),
+                    pltpu.VMEM((MARKETS, group, LANES), F32),
+                ],
+            ),
+            out_shape=jax.ShapeDtypeStruct((tile_rows, LANES), F32),
+            compiler_params=params((k_count, step_len), (k_count, step_len), (MARKETS, group, LANES), (BLOCK, step_len), (2**20,)),
+            cost_estimate=pl.CostEstimate(
+                flops=2 * cells * 256 * count // steps,
+                bytes_accessed=4 * k_count * step_len * count,
+                transcendentals=cells * count // steps,
+            ),
+            name="first_sums",
+        )(*[pltpu.with_memory_space_constraint(array, pltpu.HBM) for array in arrays])
+
+    every_draw = lax.all_to_all(
+        jnp.broadcast_to(taste_draws[None], (draw_devices, k_count, group)), "draw", 0, 0
+    )
+    denominators = first(0, steps, block_market, outside)
+    denominators, every_draw = lax.optimization_barrier((denominators, every_draw))
+
+    sums = collected([total_of(shifted(denominators, "prod", 1, prod_devices))[None]], stages)
 
     hbm_traits = pltpu.with_memory_space_constraint(product_traits, pltpu.HBM)
     traits_split = pl.pallas_call(
@@ -427,16 +443,14 @@
         name="split_products",
     )(hbm_traits, level_rows)
     draws_split = pl.pallas_call(
-        functools.partial(split_draws, len(every_draw)),
-        in_specs=[VMEM] * (1 + len(every_draw)),
+        functools.partial(split_draws, stages),
+        in_specs=[VMEM, VMEM],
         out_specs=VMEM,
         out_shape=pltpu.VMEM((depth, draws), BF16),
         compiler_params=params((k_count, draws), (depth, draws)),
         name="split_draws",
-    )(scale_row, *every_draw)
-    traits_split, draws_split = [
-        pltpu.with_memory_space_constraint(array, pltpu.VMEM) for array in (traits_split, draws_split)
-    ]
+    )(scale_row, every_draw)
+    traits_split, draws_split = near(traits_split, draws_split)
     expo = []
     for begin, end in zip(bounds, bounds[1:]):
         piece = pl.pallas_call(
@@ -450,7 +464,7 @@
             ),
             name="fill",
         )(traits_split, draws_split)
-        expo.append(pltpu.with_memory_space_constraint(piece, pltpu.VMEM))
+        expo.extend(near(piece))
     held = (traits_split, draws_split, *expo)
 
     share, partial = pl.pallas_call(
@@ -458,8 +472,8 @@
         in_specs=[SMEM] + [VMEM] * (len(sums) + 4 + len(expo)),
         out_specs=(VMEM, VMEM),
         out_shape=(
-            jax.ShapeDtypeStruct((BLOCK, LANES), F32),
-            jax.ShapeDtypeStruct((draw_devices, tile_rows, LANES), F32),
+            pltpu.VMEM((BLOCK, LANES), F32),
+            pltpu.VMEM((draw_devices, tile_rows, LANES), F32),
         ),
         scratch_shapes=[
             pltpu.VMEM((MARKETS, 8, draws), F32),
@@ -470,7 +484,7 @@
         compiler_params=held_params,
         cost_estimate=pl.CostEstimate(flops=4 * cells, bytes_accessed=2**20, transcendentals=0),
         name="both_sums",
-    )(block_market, *sums, target_rows, outside, *held)
+    )(block_market, *near(*sums), target_rows, outside, *held)
 
     parts = shifted(partial, "prod", 1, prod_devices)
     for stride, factor in stages:
@@ -489,7 +503,7 @@
         compiler_params=held_params,
         cost_estimate=pl.CostEstimate(flops=2 * cells, bytes_accessed=2**20, transcendentals=0),
         name="last_sums",
-    )(block_market, *parts, target_rows, level_rows, *held, share)
+    )(block_market, *near(*parts), target_rows, level_rows, *held, *near(share))
     return level.reshape(-1), residual.reshape(-1)
 
 

time: 93.1 us -> 86.5 us (0.929)
  local copies, waits for them, and re-layouts: 7.08 us -> 2.42 us
  Pallas kernels: 50.9 us -> 48.9 us
    ppermute x18 -> x14, starting transfers between devices: 20.9 us -> 13.5 us  [shifted(): lax.ppermute(values, axis, digit_pairs(size, stride, factor, shift))]
    all_to_all x0 -> x1, starting transfers between devices: none -> 7.25 us  [body(): lax.all_to_all(jnp.broadcast_to(taste_draws[None], (draw_devices, k_count...]
    unnamed x26 -> x4, local copies, waits for them, and re-layouts: 7.08 us -> 0.95 us
    broadcast_in_dim x0 -> x1, local copies, waits for them, and re-layouts: none -> 1.47 us  [body(): jnp.broadcast_to(taste_draws[None], (draw_devices, k_count, group))]
    pallas_call x1, Pallas kernels: 9.45 us -> 8.28 us  [body(): pl.pallas_call(functools.partial(last_sums, share_scale, stages, (len(par...]
    ppermute x18 -> x14, waiting for transfers between devices: 12.3 us -> 13.1 us  [shifted(): lax.ppermute(values, axis, digit_pairs(size, stride, factor, shift))]
  transfers between devices with their start and end apart: 18 -> 15, of which waited for: 8 -> 8; matrix products, arithmetic and copies ran while one was open for 0% -> 0% of each run, Pallas kernels for 14% -> 32%
where the time goes in v2:
time: 86.5 us; the launch traced here: 86 us
  Pallas kernels  48.9 us (57%)
  starting transfers between devices  20.8 us (24%)
  waiting for transfers between devices  13.2 us (15%)
  local copies, waits for them, and re-layouts  2.42 us (3%)
    pallas_call x1, Pallas kernels, first(): pl.pallas_call(functools.partial(first_sums, market_scale, begin), grid_s...  14.3 us
    ppermute x14, starting transfers between devices, shifted(): lax.ppermute(values, axis, digit_pairs(size, stride, factor, shift))  13.5 us
    ppermute x14, waiting for transfers between devices, shifted(): lax.ppermute(values, axis, digit_pairs(size, stride, factor, shift))  13.1 us
    pallas_call x1, Pallas kernels, body(): pl.pallas_call(functools.partial(both_sums, market_scale, share_scale, st...  13 us
    pallas_call x3, Pallas kernels, body(): pl.pallas_call(functools.partial(fill, begin), in_specs=[VMEM, VMEM], out...  10.1 us
    pallas_call x1, Pallas kernels, body(): pl.pallas_call(functools.partial(last_sums, share_scale, stages, (len(par...  8.28 us
    all_to_all x1, starting transfers between devices, body(): lax.all_to_all(jnp.broadcast_to(taste_draws[None], (draw_devices, k_count...  7.25 us
    pallas_call x1, Pallas kernels, body(): pl.pallas_call(split_products, in_specs=[ANY, VMEM], out_specs=VMEM, out_...  3.08 us
  transfers between devices with their start and end apart: 15, of which 8 were waited for; matrix products, arithmetic and copies ran while one was open for 0% of the time, Pallas kernels for 32%

profile of v2, /device:TPU:0, one launch (start us, length us, event | category | flops | bytes accessed | tf_op | source)
XLA Modules:
  0.0 86.0 jit_solution(17809190703422445982)
XLA Ops:
  0.6 1.5 %broadcast_in_dim.4 = f32[8,32,256]{2,1,0:T(8,128)} broadcast(f32[32,256]{1,0:T(8,128)} %draws_ref.1), dimensions={1,2} | broadcast | bytes 294912 | tf_op jit(solution)/shard_map/broadcast_in_dim | solution.py:428
  2.1 7.3 %all-to-all-start = ((f32[8,32,256]{2,1,0:T(8,128)}), f32[8,32,256]{2,1,0:T(8,128)S(1)}, u32[]{:S(2)}, u32[]{:S(2)}) async-start(f32[8,32,256]{2,1,0:T(8,128)} %broadcast_in_dim.4), calls=%async_computation | async-start | bytes 524288 | tf_op jit(solution)/shard_map/all_to_all | solution.py:427
  9.4 0.9 %copy-done = f32[65536]{0:T(1024)S(1)} copy-done((f32[65536]{0:T(1024)S(1)}, f32[65536]{0:T(1024)}, u32[]{:S(2)}) %copy-start) | copy-done | bytes 262168
  10.3 3.1 %split_products.1.traits_ref.refs_6_ = bf16[8192,112]{1,0:T(8,128)(2,1)S(1)} custom-call(f32[32,65536]{1,0:T(8,128)} %traits_hbm.1, f32[512,128]{1,0:T(8,128)S(1)} %bitcast.9), custom_call_target="tpu_custom_call" | custom-call | tf_op jit(solution)/shard_map/split_products/pallas_call | solution.py:436
  13.4 14.3 %first_sums.1 = f32[8,128]{1,0:T(8,128)S(1)} custom-call(s32[256]{0:T(256)} %market_ref.5, f32[32,65536]{1,0:T(8,128)} %traits_hbm.1, f32[512,128]{1,0:T(8,128)} %bitcast.7, f32[1,32]{1,0:T(1,128)} %bitcast.10, f32[32,256]{1,0:T(8,128)} %draws_ref.1, f32[4,256]{1,0:T(4,128)} %refs_5_.1), custom_call_target="tpu_custom_call" | custom-call | flops 8589934592 | bytes 8388608 | tf_op jit(solution)/shard_map/first_sums/pallas_call | solution.py:399
  27.7 0.7 collective-permute-start.2
  28.5 0.9 %collective-permute-start.1 = (f32[8,128]{1,0:T(8,128)S(1)}, f32[8,128]{1,0:T(8,128)S(1)}, u32[]{:S(2)}, u32[]{:S(2)}) collective-permute-start(f32[8,128]{1,0:T(8,128)S(1)} %first_sums.1), channel_id=1, source_target_pairs={{0,16},{8,24},{16,0},{24,8},{1,17},{9,25},{17,1},{25,9},{2,18},{10... | collective-permute-start | bytes 12296 | tf_op jit(solution)/shard_map/ppermute | solution.py:338
  29.4 0.2 collective-permute-start
  29.6 0.1 split_draws.1.right_ref.refs_7_
  29.7 3.4 %fill.5.refs_10_ = f32[8192,512]{1,0:T(8,128)S(1)} custom-call(bf16[8192,112]{1,0:T(8,128)(2,1)S(1)} %split_products.1.traits_ref.refs_6_, bf16[112,2048]{1,0:T(8,128)(2,1)S(1)} %split_draws.1.right_ref.refs_7_), custom_call_target="tpu_custom_call" | custom-call | flops 2147483648 | bytes 1048576 | tf_op jit(solution)/shard_map/fill/pallas_call | solution.py:456
  33.1 2.1 %collective-permute-start.3 = (f32[1,8,128]{2,1,0:T(8,128)S(1)}, f32[1,8,128]{2,1,0:T(8,128)S(1)}, u32[]{:S(2)}, u32[]{:S(2)}) collective-permute-start(f32[1,8,128]{2,1,0:T(8,128)S(1)} %add_bitcast_fusion), channel_id=1, source_target_pairs={{0,1},{1,0},{2,3},{3,2},{4,5},{5,4},{6,7},{7,6},{8,9},{9,8},{10,11... | collective-permute-start | bytes 12296 | tf_op jit(solution)/shard_map/ppermute | solution.py:338
  35.2 3.4 %fill.4.refs_9_ = f32[8192,512]{1,0:T(8,128)S(1)} custom-call(bf16[8192,112]{1,0:T(8,128)(2,1)S(1)} %split_products.1.traits_ref.refs_6_, bf16[112,2048]{1,0:T(8,128)(2,1)S(1)} %split_draws.1.right_ref.refs_7_), custom_call_target="tpu_custom_call" | custom-call | flops 2147483648 | bytes 1048576 | tf_op jit(solution)/shard_map/fill/pallas_call | solution.py:456
  38.6 3.3 %collective-permute-start.6 = (f32[2,8,128]{2,1,0:T(8,128)S(1)}, f32[2,8,128]{2,1,0:T(8,128)S(1)}, u32[]{:S(2)}, u32[]{:S(2)}) collective-permute-start(f32[2,8,128]{2,1,0:T(8,128)S(1)} %pad_maximum_fusion.refs_0_), channel_id=1, source_target_pairs={{0,6},{1,7},{2,0},{3,1},{4,2},{5,3},{6,4},{7,5},{8,14},{9,15},{10,... | collective-permute-start | bytes 24584 | tf_op jit(solution)/shard_map/ppermute | solution.py:338
  41.9 1.1 %collective-permute-start.4 = (f32[2,8,128]{2,1,0:T(8,128)S(1)}, f32[2,8,128]{2,1,0:T(8,128)S(1)}, u32[]{:S(2)}, u32[]{:S(2)}) collective-permute-start(f32[2,8,128]{2,1,0:T(8,128)S(1)} %pad_maximum_fusion.refs_0_), channel_id=1, source_target_pairs={{0,2},{1,3},{2,4},{3,5},{4,6},{5,7},{6,0},{7,1},{8,10},{9,11},{10,... | collective-permute-start | bytes 24584 | tf_op jit(solution)/shard_map/ppermute | solution.py:338
  43.1 3.4 %fill.3.refs_8_ = f32[8192,512]{1,0:T(8,128)S(1)} custom-call(bf16[8192,112]{1,0:T(8,128)(2,1)S(1)} %split_products.1.traits_ref.refs_6_, bf16[112,2048]{1,0:T(8,128)(2,1)S(1)} %split_draws.1.right_ref.refs_7_), custom_call_target="tpu_custom_call" | custom-call | flops 2147483648 | bytes 1048576 | tf_op jit(solution)/shard_map/fill/pallas_call | solution.py:456
  46.5 0.9 %collective-permute-done.4.refs_1_ = f32[2,8,128]{2,1,0:T(8,128)S(1)} collective-permute-done((f32[2,8,128]{2,1,0:T(8,128)S(1)}, f32[2,8,128]{2,1,0:T(8,128)S(1)}, u32[]{:S(2)}, u32[]{:S(2)}) %collective-permute-start.4) | collective-permute-done | bytes 8224 | tf_op jit(solution)/shard_map/ppermute | solution.py:338
  47.4 13.0 %both_sums.1 = (f32[256,128]{1,0:T(8,128)S(1)}, f32[8,8,128]{2,1,0:T(8,128)S(1)}) custom-call(s32[256]{0:T(256)} %market_ref.5, f32[2,8,128]{2,1,0:T(8,128)S(1)} %pad_maximum_fusion.refs_0_, f32[2,8,128]{2,1,0:T(8,128)S(1)} %collective-permute-done.4.refs_1_, f32[2,8,128]{2,1,0:T(8,128)S(1)} %collective-permute-done.5.refs_2_, ...), custom_call_target="tpu_custom_call" | custom-call | flops 67108864 | bytes 1048576 | tf_op jit(solution)/shard_map/both_sums/pallas_call | solution.py:470
  60.4 0.1 collective-permute-start.9
  60.4 0.8 collective-permute-start.8
  61.2 0.2 collective-permute-start.7
  61.4 0.7 collective-permute-done.9
  62.0 2.6 %collective-permute-done.8 = f32[8,8,128]{2,1,0:T(8,128)S(1)} collective-permute-done((f32[8,8,128]{2,1,0:T(8,128)S(1)}, f32[8,8,128]{2,1,0:T(8,128)S(1)}, u32[]{:S(2)}, u32[]{:S(2)}) %collective-permute-start.8) | collective-permute-done | bytes 32800 | tf_op jit(solution)/shard_map/ppermute | solution.py:338
  64.6 0.1 collective-permute-done.7
  64.8 0.6 collective-permute-start.10
  65.4 3.4 %collective-permute-done.10 = f32[8,8,128]{2,1,0:T(8,128)S(1)} collective-permute-done((f32[8,8,128]{2,1,0:T(8,128)S(1)}, f32[8,8,128]{2,1,0:T(8,128)S(1)}, u32[]{:S(2)}, u32[]{:S(2)}) %collective-permute-start.10) | collective-permute-done | bytes 32800 | tf_op jit(solution)/shard_map/ppermute | solution.py:338
  68.8 2.5 %collective-permute-start.13 = (f32[8,8,128]{2,1,0:T(8,128)S(1)}, f32[8,8,128]{2,1,0:T(8,128)S(1)}, u32[]{:S(2)}, u32[]{:S(2)}) collective-permute-start(f32[8,8,128]{2,1,0:T(8,128)S(1)} %add.27.refs_0_), channel_id=1, source_target_pairs={{0,6},{1,7},{2,0},{3,1},{4,2},{5,3},{6,4},{7,5},{8,14},{9,15},{10,... | collective-permute-start | bytes 98312 | tf_op jit(solution)/shard_map/ppermute | solution.py:338
  71.2 0.8 collective-permute-start.12
  72.1 0.3 collective-permute-start.11
  72.3 0.6 collective-permute-done.13.refs_3_
  72.9 3.1 %collective-permute-done.12.refs_2_ = f32[8,8,128]{2,1,0:T(8,128)S(1)} collective-permute-done((f32[8,8,128]{2,1,0:T(8,128)S(1)}, f32[8,8,128]{2,1,0:T(8,128)S(1)}, u32[]{:S(2)}, u32[]{:S(2)}) %collective-permute-start.12) | collective-permute-done | bytes 32800 | tf_op jit(solution)/shard_map/ppermute | solution.py:338
  76.1 1.7 %collective-permute-done.11.refs_1_ = f32[8,8,128]{2,1,0:T(8,128)S(1)} collective-permute-done((f32[8,8,128]{2,1,0:T(8,128)S(1)}, f32[8,8,128]{2,1,0:T(8,128)S(1)}, u32[]{:S(2)}, u32[]{:S(2)}) %collective-permute-start.11) | collective-permute-done | bytes 32800 | tf_op jit(solution)/shard_map/ppermute | solution.py:338
  77.8 8.3 %last_sums.1 = (f32[64,128]{1,0:T(8,128)}, f32[64,128]{1,0:T(8,128)}) custom-call(s32[256]{0:T(256)} %market_ref.5, f32[8,8,128]{2,1,0:T(8,128)S(1)} %add.27.refs_0_, f32[8,8,128]{2,1,0:T(8,128)S(1)} %collective-permute-done.11.refs_1_, f32[8,8,128]{2,1,0:T(8,128)S(1)} %collective-permute-done.12.refs_2_, f32[8,8,128]{2,1,0:T(8,128)S(1)} %collective-permute-done.13.refs_3_, ...), custom_call_target="tpu_custom_call" | custom-call | flops 33554432 | bytes 1048576 | tf_op jit(solution)/shard_map/last_sums/pallas_call | solution.py:493
  (15 shorter events, 0.1 us)
Async XLA Ops:
  2.1 25.6 %all-to-all-start = ((f32[8,32,256]{2,1,0:T(8,128)}), f32[8,32,256]{2,1,0:T(8,128)S(1)}, u32[]{:S(2)}, u32[]{:S(2)}) async-start(f32[8,32,256]{2,1,0:T(8,128)} %broadcast_in_dim.4), calls=%async_computation | async-start | bytes 524288 | tf_op jit(solution)/shard_map/all_to_all | solution.py:427
  9.4 0.9 %copy-start = (f32[65536]{0:T(1024)S(1)}, f32[65536]{0:T(1024)}, u32[]{:S(2)}) copy-start(f32[65536]{0:T(1024)} %param.8) | copy-start | bytes 786436
  13.4 16.2 %copy-start.1 = (f32[32]{0:T(128)S(1)}, f32[32]{0:T(128)}, u32[]{:S(2)}) copy-start(f32[32]{0:T(128)} %param.10) | copy-start | bytes 388
  27.7 5.3 %collective-permute-start.2 = (f32[8,128]{1,0:T(8,128)S(1)}, f32[8,128]{1,0:T(8,128)S(1)}, u32[]{:S(2)}, u32[]{:S(2)}) collective-permute-start(f32[8,128]{1,0:T(8,128)S(1)} %first_sums.1), channel_id=1, source_target_pairs={{0,24},{8,0},{16,8},{24,16},{1,25},{9,1},{17,9},{25,17},{2,26},{10... | collective-permute-start | bytes 12296 | tf_op jit(solution)/shard_map/ppermute | solution.py:338
  28.5 4.6 %collective-permute-start.1 = (f32[8,128]{1,0:T(8,128)S(1)}, f32[8,128]{1,0:T(8,128)S(1)}, u32[]{:S(2)}, u32[]{:S(2)}) collective-permute-start(f32[8,128]{1,0:T(8,128)S(1)} %first_sums.1), channel_id=1, source_target_pairs={{0,16},{8,24},{16,0},{24,8},{1,17},{9,25},{17,1},{25,9},{2,18},{10... | collective-permute-start | bytes 12296 | tf_op jit(solution)/shard_map/ppermute | solution.py:338
  29.4 3.7 %collective-permute-start = (f32[8,128]{1,0:T(8,128)S(1)}, f32[8,128]{1,0:T(8,128)S(1)}, u32[]{:S(2)}, u32[]{:S(2)}) collective-permute-start(f32[8,128]{1,0:T(8,128)S(1)} %first_sums.1), channel_id=1, source_target_pairs={{0,8},{8,16},{16,24},{24,0},{1,9},{9,17},{17,25},{25,1},{2,10},{10... | collective-permute-start | bytes 12296 | tf_op jit(solution)/shard_map/ppermute | solution.py:338
  33.1 5.5 %collective-permute-start.3 = (f32[1,8,128]{2,1,0:T(8,128)S(1)}, f32[1,8,128]{2,1,0:T(8,128)S(1)}, u32[]{:S(2)}, u32[]{:S(2)}) collective-permute-start(f32[1,8,128]{2,1,0:T(8,128)S(1)} %add_bitcast_fusion), channel_id=1, source_target_pairs={{0,1},{1,0},{2,3},{3,2},{4,5},{5,4},{6,7},{7,6},{8,9},{9,8},{10,11... | collective-permute-start | bytes 12296 | tf_op jit(solution)/shard_map/ppermute | solution.py:338
  38.6 7.8 %collective-permute-start.6 = (f32[2,8,128]{2,1,0:T(8,128)S(1)}, f32[2,8,128]{2,1,0:T(8,128)S(1)}, u32[]{:S(2)}, u32[]{:S(2)}) collective-permute-start(f32[2,8,128]{2,1,0:T(8,128)S(1)} %pad_maximum_fusion.refs_0_), channel_id=1, source_target_pairs={{0,6},{1,7},{2,0},{3,1},{4,2},{5,3},{6,4},{7,5},{8,14},{9,15},{10,... | collective-permute-start | bytes 24584 | tf_op jit(solution)/shard_map/ppermute | solution.py:338
  41.9 4.5 %collective-permute-start.5 = (f32[2,8,128]{2,1,0:T(8,128)S(1)}, f32[2,8,128]{2,1,0:T(8,128)S(1)}, u32[]{:S(2)}, u32[]{:S(2)}) collective-permute-start(f32[2,8,128]{2,1,0:T(8,128)S(1)} %pad_maximum_fusion.refs_0_), channel_id=1, source_target_pairs={{0,4},{1,5},{2,6},{3,7},{4,0},{5,1},{6,2},{7,3},{8,12},{9,13},{10,... | collective-permute-start | bytes 24584 | tf_op jit(solution)/shard_map/ppermute | solution.py:338
  41.9 5.4 %collective-permute-start.4 = (f32[2,8,128]{2,1,0:T(8,128)S(1)}, f32[2,8,128]{2,1,0:T(8,128)S(1)}, u32[]{:S(2)}, u32[]{:S(2)}) collective-permute-start(f32[2,8,128]{2,1,0:T(8,128)S(1)} %pad_maximum_fusion.refs_0_), channel_id=1, source_target_pairs={{0,2},{1,3},{2,4},{3,5},{4,6},{5,7},{6,0},{7,1},{8,10},{9,11},{10,... | collective-permute-start | bytes 24584 | tf_op jit(solution)/shard_map/ppermute | solution.py:338
  60.4 1.7 %collective-permute-start.9 = (f32[8,8,128]{2,1,0:T(8,128)S(1)}, f32[8,8,128]{2,1,0:T(8,128)S(1)}, u32[]{:S(2)}, u32[]{:S(2)}) collective-permute-start(f32[8,8,128]{2,1,0:T(8,128)S(1)} %get-tuple-element.10), channel_id=1, source_target_pairs={{0,24},{8,0},{16,8},{24,16},{1,25},{9,1},{17,9},{25,17},{2,26},{10... | collective-permute-start | bytes 98312 | tf_op jit(solution)/shard_map/ppermute | solution.py:338
  60.4 4.2 %collective-permute-start.8 = (f32[8,8,128]{2,1,0:T(8,128)S(1)}, f32[8,8,128]{2,1,0:T(8,128)S(1)}, u32[]{:S(2)}, u32[]{:S(2)}) collective-permute-start(f32[8,8,128]{2,1,0:T(8,128)S(1)} %get-tuple-element.10), channel_id=1, source_target_pairs={{0,16},{8,24},{16,0},{24,8},{1,17},{9,25},{17,1},{25,9},{2,18},{10... | collective-permute-start | bytes 98312 | tf_op jit(solution)/shard_map/ppermute | solution.py:338
  61.2 3.6 %collective-permute-start.7 = (f32[8,8,128]{2,1,0:T(8,128)S(1)}, f32[8,8,128]{2,1,0:T(8,128)S(1)}, u32[]{:S(2)}, u32[]{:S(2)}) collective-permute-start(f32[8,8,128]{2,1,0:T(8,128)S(1)} %get-tuple-element.10), channel_id=1, source_target_pairs={{0,8},{8,16},{16,24},{24,0},{1,9},{9,17},{17,25},{25,1},{2,10},{10... | collective-permute-start | bytes 98312 | tf_op jit(solution)/shard_map/ppermute | solution.py:338
  64.8 4.0 %collective-permute-start.10 = (f32[8,8,128]{2,1,0:T(8,128)S(1)}, f32[8,8,128]{2,1,0:T(8,128)S(1)}, u32[]{:S(2)}, u32[]{:S(2)}) collective-permute-start(f32[8,8,128]{2,1,0:T(8,128)S(1)} %add_add_fusion), channel_id=1, source_target_pairs={{0,1},{1,0},{2,3},{3,2},{4,5},{5,4},{6,7},{7,6},{8,9},{9,8},{10,11... | collective-permute-start | bytes 98312 | tf_op jit(solution)/shard_map/ppermute | solution.py:338
  68.8 4.1 %collective-permute-start.13 = (f32[8,8,128]{2,1,0:T(8,128)S(1)}, f32[8,8,128]{2,1,0:T(8,128)S(1)}, u32[]{:S(2)}, u32[]{:S(2)}) collective-permute-start(f32[8,8,128]{2,1,0:T(8,128)S(1)} %add.27.refs_0_), channel_id=1, source_target_pairs={{0,6},{1,7},{2,0},{3,1},{4,2},{5,3},{6,4},{7,5},{8,14},{9,15},{10,... | collective-permute-start | bytes 98312 | tf_op jit(solution)/shard_map/ppermute | solution.py:338
  71.2 4.8 %collective-permute-start.12 = (f32[8,8,128]{2,1,0:T(8,128)S(1)}, f32[8,8,128]{2,1,0:T(8,128)S(1)}, u32[]{:S(2)}, u32[]{:S(2)}) collective-permute-start(f32[8,8,128]{2,1,0:T(8,128)S(1)} %add.27.refs_0_), channel_id=1, source_target_pairs={{0,4},{1,5},{2,6},{3,7},{4,0},{5,1},{6,2},{7,3},{8,12},{9,13},{10,... | collective-permute-start | bytes 98312 | tf_op jit(solution)/shard_map/ppermute | solution.py:338
  72.1 5.7 %collective-permute-start.11 = (f32[8,8,128]{2,1,0:T(8,128)S(1)}, f32[8,8,128]{2,1,0:T(8,128)S(1)}, u32[]{:S(2)}, u32[]{:S(2)}) collective-permute-start(f32[8,8,128]{2,1,0:T(8,128)S(1)} %add.27.refs_0_), channel_id=1, source_target_pairs={{0,2},{1,3},{2,4},{3,5},{4,6},{5,7},{6,0},{7,1},{8,10},{9,11},{10,... | collective-permute-start | bytes 98312 | tf_op jit(solution)/shard_map/ppermute | solution.py:338

commit v3 on v2

--- a/solution.py
+++ b/solution.py
@@ -16,7 +16,7 @@
 BUDGET = 58 * 2**20
 FLOOR = 10 * 2**20
 PIECES = 3
-STEP_BLOCKS = 32
+STEP_BLOCKS = 64
 F32 = jnp.float32
 BF16 = jnp.bfloat16
 VMEM = pl.BlockSpec(memory_space=pltpu.VMEM)
@@ -122,23 +122,31 @@
         sums_ref[...] = tile if begin == 0 else tile + before_ref[...]
 
 
-def split_products(traits_hbm, level_ref, traits_out, traits_vmem, arrived):
+def split_products(traits_hbm, level_hbm, traits_out, traits_vmem, level_vmem, arrived):
     part_len = traits_vmem.shape[1]
     own = lax.axis_index("draw")
-    copy = pltpu.make_async_copy(
-        traits_hbm.at[:, pl.ds(pl.multiple_of(own * part_len, part_len), part_len)], traits_vmem, arrived
-    )
-    copy.start()
-    copy.wait()
+    rows = part_len // LANES
+    copies = (
+        pltpu.make_async_copy(
+            traits_hbm.at[:, pl.ds(pl.multiple_of(own * part_len, part_len), part_len)], traits_vmem, arrived.at[0]
+        ),
+        pltpu.make_async_copy(
+            level_hbm.at[pl.ds(pl.multiple_of(own * rows, rows), rows), :], level_vmem, arrived.at[1]
+        ),
+    )
+    for copy in copies:
+        copy.start()
+    for copy in copies:
+        copy.wait()
     blocks = part_len // BLOCK
 
     def step(block, carry):
         start = pl.multiple_of(block * BLOCK, BLOCK)
-        rows = trait_rows(traits_vmem[:, pl.ds(start, BLOCK)], level_row(level_ref, own * blocks + block))
+        rows = trait_rows(traits_vmem[:, pl.ds(start, BLOCK)], level_row(level_vmem, block))
         traits_out[pl.ds(start, BLOCK), :] = jnp.concatenate(rows, axis=0).T.astype(BF16)
         return carry
 
-    lax.fori_loop(0, blocks, step, 0, unroll=2)
+    lax.fori_loop(0, blocks, step, 0, unroll=4)
 
 
 def group_at(place, stages):
@@ -313,7 +321,7 @@
         second[...] = jnp.where(lane == block, share, second[...])
         return carry
 
-    lax.fori_loop(0, blocks, step, 0, unroll=4)
+    lax.fori_loop(0, blocks, step, 0, unroll=8)
     before = share_ref[...].T[:blocks]
     after = second[...].T[:blocks]
     residual = jnp.log(before) - jnp.log(after)
@@ -435,13 +443,17 @@
     hbm_traits = pltpu.with_memory_space_constraint(product_traits, pltpu.HBM)
     traits_split = pl.pallas_call(
         split_products,
-        in_specs=[ANY, VMEM],
+        in_specs=[ANY, ANY],
         out_specs=VMEM,
         out_shape=pltpu.VMEM((part_len, depth), BF16),
-        scratch_shapes=[pltpu.VMEM((k_count, part_len), F32), pltpu.SemaphoreType.DMA],
+        scratch_shapes=[
+            pltpu.VMEM((k_count, part_len), F32),
+            pltpu.VMEM((part_len // LANES, LANES), F32),
+            pltpu.SemaphoreType.DMA((2,)),
+        ],
         compiler_params=params((k_count, part_len), (prod_count,), (depth, part_len)),
         name="split_products",
-    )(hbm_traits, level_rows)
+    )(hbm_traits, pltpu.with_memory_space_constraint(level_rows, pltpu.HBM))
     draws_split = pl.pallas_call(
         functools.partial(split_draws, stages),
         in_specs=[VMEM, VMEM],

time: 86.5 us -> 84.2 us (0.973)
  Pallas kernels: 48.9 us -> 47.6 us
  local copies, waits for them, and re-layouts: 2.42 us -> 1.49 us
    unnamed x4 -> x2, local copies, waits for them, and re-layouts: 0.95 us -> 0.01 us
where the time goes in v3:
time: 84.2 us; the launch traced here: 83.8 us
  Pallas kernels  47.6 us (57%)
  starting transfers between devices  20.8 us (25%)
  waiting for transfers between devices  13.1 us (16%)
  local copies, waits for them, and re-layouts  1.49 us (2%)
    pallas_call x1, Pallas kernels, first(): pl.pallas_call(functools.partial(first_sums, market_scale, begin), grid_s...  14 us
    ppermute x14, starting transfers between devices, shifted(): lax.ppermute(values, axis, digit_pairs(size, stride, factor, shift))  13.5 us
    ppermute x14, waiting for transfers between devices, shifted(): lax.ppermute(values, axis, digit_pairs(size, stride, factor, shift))  13.1 us
    pallas_call x1, Pallas kernels, body(): pl.pallas_call(functools.partial(both_sums, market_scale, share_scale, st...  13 us
    pallas_call x3, Pallas kernels, body(): pl.pallas_call(functools.partial(fill, begin), in_specs=[VMEM, VMEM], out...  10.1 us
    pallas_call x1, Pallas kernels, body(): pl.pallas_call(functools.partial(last_sums, share_scale, stages, (len(par...  7.96 us
    all_to_all x1, starting transfers between devices, body(): lax.all_to_all(jnp.broadcast_to(taste_draws[None], (draw_devices, k_count...  7.25 us
    pallas_call x1, Pallas kernels, body(): pl.pallas_call(split_products, in_specs=[ANY, ANY], out_specs=VMEM, out_s...  2.43 us
  transfers between devices with their start and end apart: 15, of which 8 were waited for; matrix products, arithmetic and copies ran while one was open for 0% of the time, Pallas kernels for 32%

profile of v3, /device:TPU:0, one launch (start us, length us, event | category | flops | bytes accessed | tf_op | source)
XLA Modules:
  0.0 83.8 jit_solution(16379657151838177141)
XLA Ops:
  0.6 1.5 %broadcast_in_dim.4 = f32[8,32,256]{2,1,0:T(8,128)} broadcast(f32[32,256]{1,0:T(8,128)} %draws_ref.1), dimensions={1,2} | broadcast | bytes 294912 | tf_op jit(solution)/shard_map/broadcast_in_dim | solution.py:436
  2.1 7.3 %all-to-all-start = ((f32[8,32,256]{2,1,0:T(8,128)}), f32[8,32,256]{2,1,0:T(8,128)S(1)}, u32[]{:S(2)}, u32[]{:S(2)}) async-start(f32[8,32,256]{2,1,0:T(8,128)} %broadcast_in_dim.4), calls=%async_computation | async-start | bytes 524288 | tf_op jit(solution)/shard_map/all_to_all | solution.py:435
  9.4 2.4 %split_products.1.traits_ref.refs_6_ = bf16[8192,112]{1,0:T(8,128)(2,1)S(1)} custom-call(f32[32,65536]{1,0:T(8,128)} %traits_hbm.1, f32[512,128]{1,0:T(8,128)} %bitcast.11), custom_call_target="tpu_custom_call" | custom-call | tf_op jit(solution)/shard_map/split_products/pallas_call | solution.py:444
  11.8 14.0 %first_sums.1 = f32[8,128]{1,0:T(8,128)S(1)} custom-call(s32[256]{0:T(256)} %market_ref.5, f32[32,65536]{1,0:T(8,128)} %traits_hbm.1, f32[512,128]{1,0:T(8,128)} %bitcast.12, f32[1,32]{1,0:T(1,128)} %bitcast.7, f32[32,256]{1,0:T(8,128)} %draws_ref.1, f32[4,256]{1,0:T(4,128)} %refs_5_.1), custom_call_target="tpu_custom_call" | custom-call | flops 8589934592 | bytes 8388608 | tf_op jit(solution)/shard_map/first_sums/pallas_call | solution.py:407
  25.9 0.7 collective-permute-start.2
  26.6 0.9 %collective-permute-start.1 = (f32[8,128]{1,0:T(8,128)S(1)}, f32[8,128]{1,0:T(8,128)S(1)}, u32[]{:S(2)}, u32[]{:S(2)}) collective-permute-start(f32[8,128]{1,0:T(8,128)S(1)} %first_sums.1), channel_id=1, source_target_pairs={{0,16},{8,24},{16,0},{24,8},{1,17},{9,25},{17,1},{25,9},{2,18},{10... | collective-permute-start | bytes 12296 | tf_op jit(solution)/shard_map/ppermute | solution.py:346
  27.5 0.2 collective-permute-start
  27.7 0.1 split_draws.1.right_ref.refs_7_
  27.8 3.4 %fill.5.refs_10_ = f32[8192,512]{1,0:T(8,128)S(1)} custom-call(bf16[8192,112]{1,0:T(8,128)(2,1)S(1)} %split_products.1.traits_ref.refs_6_, bf16[112,2048]{1,0:T(8,128)(2,1)S(1)} %split_draws.1.right_ref.refs_7_), custom_call_target="tpu_custom_call" | custom-call | flops 2147483648 | bytes 1048576 | tf_op jit(solution)/shard_map/fill/pallas_call | solution.py:468
  31.2 2.1 %collective-permute-start.3 = (f32[1,8,128]{2,1,0:T(8,128)S(1)}, f32[1,8,128]{2,1,0:T(8,128)S(1)}, u32[]{:S(2)}, u32[]{:S(2)}) collective-permute-start(f32[1,8,128]{2,1,0:T(8,128)S(1)} %add_bitcast_fusion), channel_id=1, source_target_pairs={{0,1},{1,0},{2,3},{3,2},{4,5},{5,4},{6,7},{7,6},{8,9},{9,8},{10,11... | collective-permute-start | bytes 12296 | tf_op jit(solution)/shard_map/ppermute | solution.py:346
  33.3 3.4 %fill.4.refs_9_ = f32[8192,512]{1,0:T(8,128)S(1)} custom-call(bf16[8192,112]{1,0:T(8,128)(2,1)S(1)} %split_products.1.traits_ref.refs_6_, bf16[112,2048]{1,0:T(8,128)(2,1)S(1)} %split_draws.1.right_ref.refs_7_), custom_call_target="tpu_custom_call" | custom-call | flops 2147483648 | bytes 1048576 | tf_op jit(solution)/shard_map/fill/pallas_call | solution.py:468
  36.7 3.3 %collective-permute-start.6 = (f32[2,8,128]{2,1,0:T(8,128)S(1)}, f32[2,8,128]{2,1,0:T(8,128)S(1)}, u32[]{:S(2)}, u32[]{:S(2)}) collective-permute-start(f32[2,8,128]{2,1,0:T(8,128)S(1)} %pad_maximum_fusion.refs_0_), channel_id=1, source_target_pairs={{0,6},{1,7},{2,0},{3,1},{4,2},{5,3},{6,4},{7,5},{8,14},{9,15},{10,... | collective-permute-start | bytes 24584 | tf_op jit(solution)/shard_map/ppermute | solution.py:346
  40.0 1.1 %collective-permute-start.4 = (f32[2,8,128]{2,1,0:T(8,128)S(1)}, f32[2,8,128]{2,1,0:T(8,128)S(1)}, u32[]{:S(2)}, u32[]{:S(2)}) collective-permute-start(f32[2,8,128]{2,1,0:T(8,128)S(1)} %pad_maximum_fusion.refs_0_), channel_id=1, source_target_pairs={{0,2},{1,3},{2,4},{3,5},{4,6},{5,7},{6,0},{7,1},{8,10},{9,11},{10,... | collective-permute-start | bytes 24584 | tf_op jit(solution)/shard_map/ppermute | solution.py:346
  41.2 3.4 %fill.3.refs_8_ = f32[8192,512]{1,0:T(8,128)S(1)} custom-call(bf16[8192,112]{1,0:T(8,128)(2,1)S(1)} %split_products.1.traits_ref.refs_6_, bf16[112,2048]{1,0:T(8,128)(2,1)S(1)} %split_draws.1.right_ref.refs_7_), custom_call_target="tpu_custom_call" | custom-call | flops 2147483648 | bytes 1048576 | tf_op jit(solution)/shard_map/fill/pallas_call | solution.py:468
  44.5 0.0 collective-permute-done.5.refs_2_
  44.6 0.9 %collective-permute-done.4.refs_1_ = f32[2,8,128]{2,1,0:T(8,128)S(1)} collective-permute-done((f32[2,8,128]{2,1,0:T(8,128)S(1)}, f32[2,8,128]{2,1,0:T(8,128)S(1)}, u32[]{:S(2)}, u32[]{:S(2)}) %collective-permute-start.4) | collective-permute-done | bytes 8224 | tf_op jit(solution)/shard_map/ppermute | solution.py:346
  45.5 13.0 %both_sums.1 = (f32[256,128]{1,0:T(8,128)S(1)}, f32[8,8,128]{2,1,0:T(8,128)S(1)}) custom-call(s32[256]{0:T(256)} %market_ref.5, f32[2,8,128]{2,1,0:T(8,128)S(1)} %pad_maximum_fusion.refs_0_, f32[2,8,128]{2,1,0:T(8,128)S(1)} %collective-permute-done.4.refs_1_, f32[2,8,128]{2,1,0:T(8,128)S(1)} %collective-permute-done.5.refs_2_, ...), custom_call_target="tpu_custom_call" | custom-call | flops 67108864 | bytes 1048576 | tf_op jit(solution)/shard_map/both_sums/pallas_call | solution.py:482
  58.5 0.1 collective-permute-start.9
  58.5 0.7 collective-permute-start.8
  59.3 0.2 collective-permute-start.7
  59.4 0.7 collective-permute-done.9
  60.1 2.6 %collective-permute-done.8 = f32[8,8,128]{2,1,0:T(8,128)S(1)} collective-permute-done((f32[8,8,128]{2,1,0:T(8,128)S(1)}, f32[8,8,128]{2,1,0:T(8,128)S(1)}, u32[]{:S(2)}, u32[]{:S(2)}) %collective-permute-start.8) | collective-permute-done | bytes 32800 | tf_op jit(solution)/shard_map/ppermute | solution.py:346
  62.7 0.1 collective-permute-done.7
  62.9 0.6 collective-permute-start.10
  63.5 3.3 %collective-permute-done.10 = f32[8,8,128]{2,1,0:T(8,128)S(1)} collective-permute-done((f32[8,8,128]{2,1,0:T(8,128)S(1)}, f32[8,8,128]{2,1,0:T(8,128)S(1)}, u32[]{:S(2)}, u32[]{:S(2)}) %collective-permute-start.10) | collective-permute-done | bytes 32800 | tf_op jit(solution)/shard_map/ppermute | solution.py:346
  66.8 2.5 %collective-permute-start.13 = (f32[8,8,128]{2,1,0:T(8,128)S(1)}, f32[8,8,128]{2,1,0:T(8,128)S(1)}, u32[]{:S(2)}, u32[]{:S(2)}) collective-permute-start(f32[8,8,128]{2,1,0:T(8,128)S(1)} %add.27.refs_0_), channel_id=1, source_target_pairs={{0,6},{1,7},{2,0},{3,1},{4,2},{5,3},{6,4},{7,5},{8,14},{9,15},{10,... | collective-permute-start | bytes 98312 | tf_op jit(solution)/shard_map/ppermute | solution.py:346
  69.3 0.8 %collective-permute-start.12 = (f32[8,8,128]{2,1,0:T(8,128)S(1)}, f32[8,8,128]{2,1,0:T(8,128)S(1)}, u32[]{:S(2)}, u32[]{:S(2)}) collective-permute-start(f32[8,8,128]{2,1,0:T(8,128)S(1)} %add.27.refs_0_), channel_id=1, source_target_pairs={{0,4},{1,5},{2,6},{3,7},{4,0},{5,1},{6,2},{7,3},{8,12},{9,13},{10,... | collective-permute-start | bytes 98312 | tf_op jit(solution)/shard_map/ppermute | solution.py:346
  70.1 0.3 collective-permute-start.11
  70.4 0.5 collective-permute-done.13.refs_3_
  71.0 3.1 %collective-permute-done.12.refs_2_ = f32[8,8,128]{2,1,0:T(8,128)S(1)} collective-permute-done((f32[8,8,128]{2,1,0:T(8,128)S(1)}, f32[8,8,128]{2,1,0:T(8,128)S(1)}, u32[]{:S(2)}, u32[]{:S(2)}) %collective-permute-start.12) | collective-permute-done | bytes 32800 | tf_op jit(solution)/shard_map/ppermute | solution.py:346
  74.1 1.7 %collective-permute-done.11.refs_1_ = f32[8,8,128]{2,1,0:T(8,128)S(1)} collective-permute-done((f32[8,8,128]{2,1,0:T(8,128)S(1)}, f32[8,8,128]{2,1,0:T(8,128)S(1)}, u32[]{:S(2)}, u32[]{:S(2)}) %collective-permute-start.11) | collective-permute-done | bytes 32800 | tf_op jit(solution)/shard_map/ppermute | solution.py:346
  75.9 8.0 %last_sums.1 = (f32[64,128]{1,0:T(8,128)}, f32[64,128]{1,0:T(8,128)}) custom-call(s32[256]{0:T(256)} %market_ref.5, f32[8,8,128]{2,1,0:T(8,128)S(1)} %add.27.refs_0_, f32[8,8,128]{2,1,0:T(8,128)S(1)} %collective-permute-done.11.refs_1_, f32[8,8,128]{2,1,0:T(8,128)S(1)} %collective-permute-done.12.refs_2_, f32[8,8,128]{2,1,0:T(8,128)S(1)} %collective-permute-done.13.refs_3_, ...), custom_call_target="tpu_custom_call" | custom-call | flops 33554432 | bytes 1048576 | tf_op jit(solution)/shard_map/last_sums/pallas_call | solution.py:505
  (13 shorter events, 0.1 us)
Async XLA Ops:
  2.1 23.7 %all-to-all-start = ((f32[8,32,256]{2,1,0:T(8,128)}), f32[8,32,256]{2,1,0:T(8,128)S(1)}, u32[]{:S(2)}, u32[]{:S(2)}) async-start(f32[8,32,256]{2,1,0:T(8,128)} %broadcast_in_dim.4), calls=%async_computation | async-start | bytes 524288 | tf_op jit(solution)/shard_map/all_to_all | solution.py:435
  11.8 15.9 %copy-start = (f32[32]{0:T(128)S(1)}, f32[32]{0:T(128)}, u32[]{:S(2)}) copy-start(f32[32]{0:T(128)} %param.10) | copy-start | bytes 388
  25.9 5.3 %collective-permute-start.2 = (f32[8,128]{1,0:T(8,128)S(1)}, f32[8,128]{1,0:T(8,128)S(1)}, u32[]{:S(2)}, u32[]{:S(2)}) collective-permute-start(f32[8,128]{1,0:T(8,128)S(1)} %first_sums.1), channel_id=1, source_target_pairs={{0,24},{8,0},{16,8},{24,16},{1,25},{9,1},{17,9},{25,17},{2,26},{10... | collective-permute-start | bytes 12296 | tf_op jit(solution)/shard_map/ppermute | solution.py:346
  26.6 4.6 %collective-permute-start.1 = (f32[8,128]{1,0:T(8,128)S(1)}, f32[8,128]{1,0:T(8,128)S(1)}, u32[]{:S(2)}, u32[]{:S(2)}) collective-permute-start(f32[8,128]{1,0:T(8,128)S(1)} %first_sums.1), channel_id=1, source_target_pairs={{0,16},{8,24},{16,0},{24,8},{1,17},{9,25},{17,1},{25,9},{2,18},{10... | collective-permute-start | bytes 12296 | tf_op jit(solution)/shard_map/ppermute | solution.py:346
  27.5 3.7 %collective-permute-start = (f32[8,128]{1,0:T(8,128)S(1)}, f32[8,128]{1,0:T(8,128)S(1)}, u32[]{:S(2)}, u32[]{:S(2)}) collective-permute-start(f32[8,128]{1,0:T(8,128)S(1)} %first_sums.1), channel_id=1, source_target_pairs={{0,8},{8,16},{16,24},{24,0},{1,9},{9,17},{17,25},{25,1},{2,10},{10... | collective-permute-start | bytes 12296 | tf_op jit(solution)/shard_map/ppermute | solution.py:346
  31.2 5.5 %collective-permute-start.3 = (f32[1,8,128]{2,1,0:T(8,128)S(1)}, f32[1,8,128]{2,1,0:T(8,128)S(1)}, u32[]{:S(2)}, u32[]{:S(2)}) collective-permute-start(f32[1,8,128]{2,1,0:T(8,128)S(1)} %add_bitcast_fusion), channel_id=1, source_target_pairs={{0,1},{1,0},{2,3},{3,2},{4,5},{5,4},{6,7},{7,6},{8,9},{9,8},{10,11... | collective-permute-start | bytes 12296 | tf_op jit(solution)/shard_map/ppermute | solution.py:346
  36.7 7.8 %collective-permute-start.6 = (f32[2,8,128]{2,1,0:T(8,128)S(1)}, f32[2,8,128]{2,1,0:T(8,128)S(1)}, u32[]{:S(2)}, u32[]{:S(2)}) collective-permute-start(f32[2,8,128]{2,1,0:T(8,128)S(1)} %pad_maximum_fusion.refs_0_), channel_id=1, source_target_pairs={{0,6},{1,7},{2,0},{3,1},{4,2},{5,3},{6,4},{7,5},{8,14},{9,15},{10,... | collective-permute-start | bytes 24584 | tf_op jit(solution)/shard_map/ppermute | solution.py:346
  40.0 4.5 %collective-permute-start.5 = (f32[2,8,128]{2,1,0:T(8,128)S(1)}, f32[2,8,128]{2,1,0:T(8,128)S(1)}, u32[]{:S(2)}, u32[]{:S(2)}) collective-permute-start(f32[2,8,128]{2,1,0:T(8,128)S(1)} %pad_maximum_fusion.refs_0_), channel_id=1, source_target_pairs={{0,4},{1,5},{2,6},{3,7},{4,0},{5,1},{6,2},{7,3},{8,12},{9,13},{10,... | collective-permute-start | bytes 24584 | tf_op jit(solution)/shard_map/ppermute | solution.py:346
  40.0 5.4 %collective-permute-start.4 = (f32[2,8,128]{2,1,0:T(8,128)S(1)}, f32[2,8,128]{2,1,0:T(8,128)S(1)}, u32[]{:S(2)}, u32[]{:S(2)}) collective-permute-start(f32[2,8,128]{2,1,0:T(8,128)S(1)} %pad_maximum_fusion.refs_0_), channel_id=1, source_target_pairs={{0,2},{1,3},{2,4},{3,5},{4,6},{5,7},{6,0},{7,1},{8,10},{9,11},{10,... | collective-permute-start | bytes 24584 | tf_op jit(solution)/shard_map/ppermute | solution.py:346
  58.5 1.7 %collective-permute-start.9 = (f32[8,8,128]{2,1,0:T(8,128)S(1)}, f32[8,8,128]{2,1,0:T(8,128)S(1)}, u32[]{:S(2)}, u32[]{:S(2)}) collective-permute-start(f32[8,8,128]{2,1,0:T(8,128)S(1)} %get-tuple-element.10), channel_id=1, source_target_pairs={{0,24},{8,0},{16,8},{24,16},{1,25},{9,1},{17,9},{25,17},{2,26},{10... | collective-permute-start | bytes 98312 | tf_op jit(solution)/shard_map/ppermute | solution.py:346
  58.5 4.2 %collective-permute-start.8 = (f32[8,8,128]{2,1,0:T(8,128)S(1)}, f32[8,8,128]{2,1,0:T(8,128)S(1)}, u32[]{:S(2)}, u32[]{:S(2)}) collective-permute-start(f32[8,8,128]{2,1,0:T(8,128)S(1)} %get-tuple-element.10), channel_id=1, source_target_pairs={{0,16},{8,24},{16,0},{24,8},{1,17},{9,25},{17,1},{25,9},{2,18},{10... | collective-permute-start | bytes 98312 | tf_op jit(solution)/shard_map/ppermute | solution.py:346
  59.3 3.6 %collective-permute-start.7 = (f32[8,8,128]{2,1,0:T(8,128)S(1)}, f32[8,8,128]{2,1,0:T(8,128)S(1)}, u32[]{:S(2)}, u32[]{:S(2)}) collective-permute-start(f32[8,8,128]{2,1,0:T(8,128)S(1)} %get-tuple-element.10), channel_id=1, source_target_pairs={{0,8},{8,16},{16,24},{24,0},{1,9},{9,17},{17,25},{25,1},{2,10},{10... | collective-permute-start | bytes 98312 | tf_op jit(solution)/shard_map/ppermute | solution.py:346
  62.9 4.0 %collective-permute-start.10 = (f32[8,8,128]{2,1,0:T(8,128)S(1)}, f32[8,8,128]{2,1,0:T(8,128)S(1)}, u32[]{:S(2)}, u32[]{:S(2)}) collective-permute-start(f32[8,8,128]{2,1,0:T(8,128)S(1)} %add_add_fusion), channel_id=1, source_target_pairs={{0,1},{1,0},{2,3},{3,2},{4,5},{5,4},{6,7},{7,6},{8,9},{9,8},{10,11... | collective-permute-start | bytes 98312 | tf_op jit(solution)/shard_map/ppermute | solution.py:346
  66.8 4.1 %collective-permute-start.13 = (f32[8,8,128]{2,1,0:T(8,128)S(1)}, f32[8,8,128]{2,1,0:T(8,128)S(1)}, u32[]{:S(2)}, u32[]{:S(2)}) collective-permute-start(f32[8,8,128]{2,1,0:T(8,128)S(1)} %add.27.refs_0_), channel_id=1, source_target_pairs={{0,6},{1,7},{2,0},{3,1},{4,2},{5,3},{6,4},{7,5},{8,14},{9,15},{10,... | collective-permute-start | bytes 98312 | tf_op jit(solution)/shard_map/ppermute | solution.py:346
  69.3 4.8 %collective-permute-start.12 = (f32[8,8,128]{2,1,0:T(8,128)S(1)}, f32[8,8,128]{2,1,0:T(8,128)S(1)}, u32[]{:S(2)}, u32[]{:S(2)}) collective-permute-start(f32[8,8,128]{2,1,0:T(8,128)S(1)} %add.27.refs_0_), channel_id=1, source_target_pairs={{0,4},{1,5},{2,6},{3,7},{4,0},{5,1},{6,2},{7,3},{8,12},{9,13},{10,... | collective-permute-start | bytes 98312 | tf_op jit(solution)/shard_map/ppermute | solution.py:346
  70.1 5.7 %collective-permute-start.11 = (f32[8,8,128]{2,1,0:T(8,128)S(1)}, f32[8,8,128]{2,1,0:T(8,128)S(1)}, u32[]{:S(2)}, u32[]{:S(2)}) collective-permute-start(f32[8,8,128]{2,1,0:T(8,128)S(1)} %add.27.refs_0_), channel_id=1, source_target_pairs={{0,2},{1,3},{2,4},{3,5},{4,6},{5,7},{6,0},{7,1},{8,10},{9,11},{10,... | collective-permute-start | bytes 98312 | tf_op jit(solution)/shard_map/ppermute | solution.py:346

commit v4 on v3

--- a/solution.py
+++ b/solution.py
@@ -189,7 +189,7 @@
             lax.fori_loop(0, kept // 256, inner, 0)
         return carry
 
-    lax.fori_loop(0, blocks, step, 0, unroll=4)
+    lax.fori_loop(0, blocks, step, 0, unroll=16)
 
 
 def inverse_rows(inverse, pieces):

time: 84.2 us -> 81.5 us (0.968)
  Pallas kernels: 47.6 us -> 44.9 us
    pallas_call x3, Pallas kernels: 10.1 us -> 7.39 us  [body(): pl.pallas_call(functools.partial(fill, begin), in_specs=[VMEM, VMEM], out...]
  transfers between devices with their start and end apart: 15 -> 15, of which waited for: 8 -> 10; matrix products, arithmetic and copies ran while one was open for 0% -> 0% of each run, Pallas kernels for 32% -> 30%
where the time goes in v4:
time: 81.5 us; the launch traced here: 81.1 us
  Pallas kernels  44.9 us (55%)
  starting transfers between devices  20.9 us (26%)
  waiting for transfers between devices  13 us (16%)
  local copies, waits for them, and re-layouts  1.49 us (2%)
    pallas_call x1, Pallas kernels, first(): pl.pallas_call(functools.partial(first_sums, market_scale, begin), grid_s...  14 us
    ppermute x14, starting transfers between devices, shifted(): lax.ppermute(values, axis, digit_pairs(size, stride, factor, shift))  13.7 us
    ppermute x14, waiting for transfers between devices, shifted(): lax.ppermute(values, axis, digit_pairs(size, stride, factor, shift))  13 us
    pallas_call x1, Pallas kernels, body(): pl.pallas_call(functools.partial(both_sums, market_scale, share_scale, st...  12.9 us
    pallas_call x1, Pallas kernels, body(): pl.pallas_call(functools.partial(last_sums, share_scale, stages, (len(par...  7.98 us
    pallas_call x3, Pallas kernels, body(): pl.pallas_call(functools.partial(fill, begin), in_specs=[VMEM, VMEM], out...  7.39 us
    all_to_all x1, starting transfers between devices, body(): lax.all_to_all(jnp.broadcast_to(taste_draws[None], (draw_devices, k_count...  7.25 us
    pallas_call x1, Pallas kernels, body(): pl.pallas_call(split_products, in_specs=[ANY, ANY], out_specs=VMEM, out_s...  2.43 us
  transfers between devices with their start and end apart: 15, of which 10 were waited for; matrix products, arithmetic and copies ran while one was open for 0% of the time, Pallas kernels for 30%

profile of v4, /device:TPU:0, one launch (start us, length us, event | category | flops | bytes accessed | tf_op | source)
XLA Modules:
  0.0 81.1 jit_solution(18296561105879105622)
XLA Ops:
  0.6 1.5 %broadcast_in_dim.4 = f32[8,32,256]{2,1,0:T(8,128)} broadcast(f32[32,256]{1,0:T(8,128)} %draws_ref.1), dimensions={1,2} | broadcast | bytes 294912 | tf_op jit(solution)/shard_map/broadcast_in_dim | solution.py:436
  2.1 7.3 %all-to-all-start = ((f32[8,32,256]{2,1,0:T(8,128)}), f32[8,32,256]{2,1,0:T(8,128)S(1)}, u32[]{:S(2)}, u32[]{:S(2)}) async-start(f32[8,32,256]{2,1,0:T(8,128)} %broadcast_in_dim.4), calls=%async_computation | async-start | bytes 524288 | tf_op jit(solution)/shard_map/all_to_all | solution.py:435
  9.4 2.4 %split_products.1.traits_ref.refs_6_ = bf16[8192,112]{1,0:T(8,128)(2,1)S(1)} custom-call(f32[32,65536]{1,0:T(8,128)} %traits_hbm.1, f32[512,128]{1,0:T(8,128)} %bitcast.11), custom_call_target="tpu_custom_call" | custom-call | tf_op jit(solution)/shard_map/split_products/pallas_call | solution.py:444
  11.8 14.0 %first_sums.1 = f32[8,128]{1,0:T(8,128)S(1)} custom-call(s32[256]{0:T(256)} %market_ref.5, f32[32,65536]{1,0:T(8,128)} %traits_hbm.1, f32[512,128]{1,0:T(8,128)} %bitcast.12, f32[1,32]{1,0:T(1,128)} %bitcast.7, f32[32,256]{1,0:T(8,128)} %draws_ref.1, f32[4,256]{1,0:T(4,128)} %refs_5_.1), custom_call_target="tpu_custom_call" | custom-call | flops 8589934592 | bytes 8388608 | tf_op jit(solution)/shard_map/first_sums/pallas_call | solution.py:407
  25.9 0.7 collective-permute-start.2
  26.6 0.9 %collective-permute-start.1 = (f32[8,128]{1,0:T(8,128)S(1)}, f32[8,128]{1,0:T(8,128)S(1)}, u32[]{:S(2)}, u32[]{:S(2)}) collective-permute-start(f32[8,128]{1,0:T(8,128)S(1)} %first_sums.1), channel_id=1, source_target_pairs={{0,16},{8,24},{16,0},{24,8},{1,17},{9,25},{17,1},{25,9},{2,18},{10... | collective-permute-start | bytes 12296 | tf_op jit(solution)/shard_map/ppermute | solution.py:346
  27.5 0.2 collective-permute-start
  27.7 0.1 split_draws.1.right_ref.refs_7_
  27.8 2.5 %fill.5.refs_10_ = f32[8192,512]{1,0:T(8,128)S(1)} custom-call(bf16[8192,112]{1,0:T(8,128)(2,1)S(1)} %split_products.1.traits_ref.refs_6_, bf16[112,2048]{1,0:T(8,128)(2,1)S(1)} %split_draws.1.right_ref.refs_7_), custom_call_target="tpu_custom_call" | custom-call | flops 2147483648 | bytes 1048576 | tf_op jit(solution)/shard_map/fill/pallas_call | solution.py:468
  30.3 0.2 collective-permute-done
  30.5 2.0 %collective-permute-start.3 = (f32[1,8,128]{2,1,0:T(8,128)S(1)}, f32[1,8,128]{2,1,0:T(8,128)S(1)}, u32[]{:S(2)}, u32[]{:S(2)}) collective-permute-start(f32[1,8,128]{2,1,0:T(8,128)S(1)} %add_bitcast_fusion), channel_id=1, source_target_pairs={{0,1},{1,0},{2,3},{3,2},{4,5},{5,4},{6,7},{7,6},{8,9},{9,8},{10,11... | collective-permute-start | bytes 12296 | tf_op jit(solution)/shard_map/ppermute | solution.py:346
  32.5 2.5 %fill.4.refs_9_ = f32[8192,512]{1,0:T(8,128)S(1)} custom-call(bf16[8192,112]{1,0:T(8,128)(2,1)S(1)} %split_products.1.traits_ref.refs_6_, bf16[112,2048]{1,0:T(8,128)(2,1)S(1)} %split_draws.1.right_ref.refs_7_), custom_call_target="tpu_custom_call" | custom-call | flops 2147483648 | bytes 1048576 | tf_op jit(solution)/shard_map/fill/pallas_call | solution.py:468
  35.1 3.3 %collective-permute-start.6 = (f32[2,8,128]{2,1,0:T(8,128)S(1)}, f32[2,8,128]{2,1,0:T(8,128)S(1)}, u32[]{:S(2)}, u32[]{:S(2)}) collective-permute-start(f32[2,8,128]{2,1,0:T(8,128)S(1)} %pad_maximum_fusion.refs_0_), channel_id=1, source_target_pairs={{0,6},{1,7},{2,0},{3,1},{4,2},{5,3},{6,4},{7,5},{8,14},{9,15},{10,... | collective-permute-start | bytes 24584 | tf_op jit(solution)/shard_map/ppermute | solution.py:346
  38.4 1.1 %collective-permute-start.4 = (f32[2,8,128]{2,1,0:T(8,128)S(1)}, f32[2,8,128]{2,1,0:T(8,128)S(1)}, u32[]{:S(2)}, u32[]{:S(2)}) collective-permute-start(f32[2,8,128]{2,1,0:T(8,128)S(1)} %pad_maximum_fusion.refs_0_), channel_id=1, source_target_pairs={{0,2},{1,3},{2,4},{3,5},{4,6},{5,7},{6,0},{7,1},{8,10},{9,11},{10,... | collective-permute-start | bytes 24584 | tf_op jit(solution)/shard_map/ppermute | solution.py:346
  39.5 2.5 %fill.3.refs_8_ = f32[8192,512]{1,0:T(8,128)S(1)} custom-call(bf16[8192,112]{1,0:T(8,128)(2,1)S(1)} %split_products.1.traits_ref.refs_6_, bf16[112,2048]{1,0:T(8,128)(2,1)S(1)} %split_draws.1.right_ref.refs_7_), custom_call_target="tpu_custom_call" | custom-call | flops 2147483648 | bytes 1048576 | tf_op jit(solution)/shard_map/fill/pallas_call | solution.py:468
  42.0 1.0 %collective-permute-done.5.refs_2_ = f32[2,8,128]{2,1,0:T(8,128)S(1)} collective-permute-done((f32[2,8,128]{2,1,0:T(8,128)S(1)}, f32[2,8,128]{2,1,0:T(8,128)S(1)}, u32[]{:S(2)}, u32[]{:S(2)}) %collective-permute-start.5) | collective-permute-done | bytes 8224 | tf_op jit(solution)/shard_map/ppermute | solution.py:346
  43.0 0.8 %collective-permute-done.4.refs_1_ = f32[2,8,128]{2,1,0:T(8,128)S(1)} collective-permute-done((f32[2,8,128]{2,1,0:T(8,128)S(1)}, f32[2,8,128]{2,1,0:T(8,128)S(1)}, u32[]{:S(2)}, u32[]{:S(2)}) %collective-permute-start.4) | collective-permute-done | bytes 8224 | tf_op jit(solution)/shard_map/ppermute | solution.py:346
  43.8 12.9 %both_sums.1 = (f32[256,128]{1,0:T(8,128)S(1)}, f32[8,8,128]{2,1,0:T(8,128)S(1)}) custom-call(s32[256]{0:T(256)} %market_ref.5, f32[2,8,128]{2,1,0:T(8,128)S(1)} %pad_maximum_fusion.refs_0_, f32[2,8,128]{2,1,0:T(8,128)S(1)} %collective-permute-done.4.refs_1_, f32[2,8,128]{2,1,0:T(8,128)S(1)} %collective-permute-done.5.refs_2_, ...), custom_call_target="tpu_custom_call" | custom-call | flops 67108864 | bytes 1048576 | tf_op jit(solution)/shard_map/both_sums/pallas_call | solution.py:482
  56.9 0.9 %collective-permute-start.8 = (f32[8,8,128]{2,1,0:T(8,128)S(1)}, f32[8,8,128]{2,1,0:T(8,128)S(1)}, u32[]{:S(2)}, u32[]{:S(2)}) collective-permute-start(f32[8,8,128]{2,1,0:T(8,128)S(1)} %get-tuple-element.10), channel_id=1, source_target_pairs={{0,16},{8,24},{16,0},{24,8},{1,17},{9,25},{17,1},{25,9},{2,18},{10... | collective-permute-start | bytes 98312 | tf_op jit(solution)/shard_map/ppermute | solution.py:346
  57.7 0.2 collective-permute-start.7
  57.9 0.5 collective-permute-done.9
  58.4 2.5 %collective-permute-done.8 = f32[8,8,128]{2,1,0:T(8,128)S(1)} collective-permute-done((f32[8,8,128]{2,1,0:T(8,128)S(1)}, f32[8,8,128]{2,1,0:T(8,128)S(1)}, u32[]{:S(2)}, u32[]{:S(2)}) %collective-permute-start.8) | collective-permute-done | bytes 32800 | tf_op jit(solution)/shard_map/ppermute | solution.py:346
  60.9 0.3 collective-permute-done.7
  61.2 1.1 %collective-permute-start.10 = (f32[8,8,128]{2,1,0:T(8,128)S(1)}, f32[8,8,128]{2,1,0:T(8,128)S(1)}, u32[]{:S(2)}, u32[]{:S(2)}) collective-permute-start(f32[8,8,128]{2,1,0:T(8,128)S(1)} %add_add_fusion), channel_id=1, source_target_pairs={{0,1},{1,0},{2,3},{3,2},{4,5},{5,4},{6,7},{7,6},{8,9},{9,8},{10,11... | collective-permute-start | bytes 98312 | tf_op jit(solution)/shard_map/ppermute | solution.py:346
  62.3 2.9 %collective-permute-done.10 = f32[8,8,128]{2,1,0:T(8,128)S(1)} collective-permute-done((f32[8,8,128]{2,1,0:T(8,128)S(1)}, f32[8,8,128]{2,1,0:T(8,128)S(1)}, u32[]{:S(2)}, u32[]{:S(2)}) %collective-permute-start.10) | collective-permute-done | bytes 32800 | tf_op jit(solution)/shard_map/ppermute | solution.py:346
  65.2 1.4 %collective-permute-start.13 = (f32[8,8,128]{2,1,0:T(8,128)S(1)}, f32[8,8,128]{2,1,0:T(8,128)S(1)}, u32[]{:S(2)}, u32[]{:S(2)}) collective-permute-start(f32[8,8,128]{2,1,0:T(8,128)S(1)} %add.27.refs_0_), channel_id=1, source_target_pairs={{0,6},{1,7},{2,0},{3,1},{4,2},{5,3},{6,4},{7,5},{8,14},{9,15},{10,... | collective-permute-start | bytes 98312 | tf_op jit(solution)/shard_map/ppermute | solution.py:346
  66.6 0.8 %collective-permute-start.12 = (f32[8,8,128]{2,1,0:T(8,128)S(1)}, f32[8,8,128]{2,1,0:T(8,128)S(1)}, u32[]{:S(2)}, u32[]{:S(2)}) collective-permute-start(f32[8,8,128]{2,1,0:T(8,128)S(1)} %add.27.refs_0_), channel_id=1, source_target_pairs={{0,4},{1,5},{2,6},{3,7},{4,0},{5,1},{6,2},{7,3},{8,12},{9,13},{10,... | collective-permute-start | bytes 98312 | tf_op jit(solution)/shard_map/ppermute | solution.py:346
  67.4 0.9 %collective-permute-start.11 = (f32[8,8,128]{2,1,0:T(8,128)S(1)}, f32[8,8,128]{2,1,0:T(8,128)S(1)}, u32[]{:S(2)}, u32[]{:S(2)}) collective-permute-start(f32[8,8,128]{2,1,0:T(8,128)S(1)} %add.27.refs_0_), channel_id=1, source_target_pairs={{0,2},{1,3},{2,4},{3,5},{4,6},{5,7},{6,0},{7,1},{8,10},{9,11},{10,... | collective-permute-start | bytes 98312 | tf_op jit(solution)/shard_map/ppermute | solution.py:346
  68.3 0.8 collective-permute-done.13.refs_3_
  69.1 2.6 %collective-permute-done.12.refs_2_ = f32[8,8,128]{2,1,0:T(8,128)S(1)} collective-permute-done((f32[8,8,128]{2,1,0:T(8,128)S(1)}, f32[8,8,128]{2,1,0:T(8,128)S(1)}, u32[]{:S(2)}, u32[]{:S(2)}) %collective-permute-start.12) | collective-permute-done | bytes 32800 | tf_op jit(solution)/shard_map/ppermute | solution.py:346
  71.7 1.4 %collective-permute-done.11.refs_1_ = f32[8,8,128]{2,1,0:T(8,128)S(1)} collective-permute-done((f32[8,8,128]{2,1,0:T(8,128)S(1)}, f32[8,8,128]{2,1,0:T(8,128)S(1)}, u32[]{:S(2)}, u32[]{:S(2)}) %collective-permute-start.11) | collective-permute-done | bytes 32800 | tf_op jit(solution)/shard_map/ppermute | solution.py:346
  73.1 8.0 %last_sums.1 = (f32[64,128]{1,0:T(8,128)}, f32[64,128]{1,0:T(8,128)}) custom-call(s32[256]{0:T(256)} %market_ref.5, f32[8,8,128]{2,1,0:T(8,128)S(1)} %add.27.refs_0_, f32[8,8,128]{2,1,0:T(8,128)S(1)} %collective-permute-done.11.refs_1_, f32[8,8,128]{2,1,0:T(8,128)S(1)} %collective-permute-done.12.refs_2_, f32[8,8,128]{2,1,0:T(8,128)S(1)} %collective-permute-done.13.refs_3_, ...), custom_call_target="tpu_custom_call" | custom-call | flops 33554432 | bytes 1048576 | tf_op jit(solution)/shard_map/last_sums/pallas_call | solution.py:505
  (13 shorter events, 0.1 us)
Async XLA Ops:
  2.1 23.7 %all-to-all-start = ((f32[8,32,256]{2,1,0:T(8,128)}), f32[8,32,256]{2,1,0:T(8,128)S(1)}, u32[]{:S(2)}, u32[]{:S(2)}) async-start(f32[8,32,256]{2,1,0:T(8,128)} %broadcast_in_dim.4), calls=%async_computation | async-start | bytes 524288 | tf_op jit(solution)/shard_map/all_to_all | solution.py:435
  11.8 15.9 %copy-start = (f32[32]{0:T(128)S(1)}, f32[32]{0:T(128)}, u32[]{:S(2)}) copy-start(f32[32]{0:T(128)} %param.10) | copy-start | bytes 388
  25.9 4.4 %collective-permute-start.2 = (f32[8,128]{1,0:T(8,128)S(1)}, f32[8,128]{1,0:T(8,128)S(1)}, u32[]{:S(2)}, u32[]{:S(2)}) collective-permute-start(f32[8,128]{1,0:T(8,128)S(1)} %first_sums.1), channel_id=1, source_target_pairs={{0,24},{8,0},{16,8},{24,16},{1,25},{9,1},{17,9},{25,17},{2,26},{10... | collective-permute-start | bytes 12296 | tf_op jit(solution)/shard_map/ppermute | solution.py:346
  26.6 3.7 %collective-permute-start.1 = (f32[8,128]{1,0:T(8,128)S(1)}, f32[8,128]{1,0:T(8,128)S(1)}, u32[]{:S(2)}, u32[]{:S(2)}) collective-permute-start(f32[8,128]{1,0:T(8,128)S(1)} %first_sums.1), channel_id=1, source_target_pairs={{0,16},{8,24},{16,0},{24,8},{1,17},{9,25},{17,1},{25,9},{2,18},{10... | collective-permute-start | bytes 12296 | tf_op jit(solution)/shard_map/ppermute | solution.py:346
  27.5 3.0 %collective-permute-start = (f32[8,128]{1,0:T(8,128)S(1)}, f32[8,128]{1,0:T(8,128)S(1)}, u32[]{:S(2)}, u32[]{:S(2)}) collective-permute-start(f32[8,128]{1,0:T(8,128)S(1)} %first_sums.1), channel_id=1, source_target_pairs={{0,8},{8,16},{16,24},{24,0},{1,9},{9,17},{17,25},{25,1},{2,10},{10... | collective-permute-start | bytes 12296 | tf_op jit(solution)/shard_map/ppermute | solution.py:346
  30.5 4.5 %collective-permute-start.3 = (f32[1,8,128]{2,1,0:T(8,128)S(1)}, f32[1,8,128]{2,1,0:T(8,128)S(1)}, u32[]{:S(2)}, u32[]{:S(2)}) collective-permute-start(f32[1,8,128]{2,1,0:T(8,128)S(1)} %add_bitcast_fusion), channel_id=1, source_target_pairs={{0,1},{1,0},{2,3},{3,2},{4,5},{5,4},{6,7},{7,6},{8,9},{9,8},{10,11... | collective-permute-start | bytes 12296 | tf_op jit(solution)/shard_map/ppermute | solution.py:346
  35.1 6.9 %collective-permute-start.6 = (f32[2,8,128]{2,1,0:T(8,128)S(1)}, f32[2,8,128]{2,1,0:T(8,128)S(1)}, u32[]{:S(2)}, u32[]{:S(2)}) collective-permute-start(f32[2,8,128]{2,1,0:T(8,128)S(1)} %pad_maximum_fusion.refs_0_), channel_id=1, source_target_pairs={{0,6},{1,7},{2,0},{3,1},{4,2},{5,3},{6,4},{7,5},{8,14},{9,15},{10,... | collective-permute-start | bytes 24584 | tf_op jit(solution)/shard_map/ppermute | solution.py:346
  38.4 4.6 %collective-permute-start.5 = (f32[2,8,128]{2,1,0:T(8,128)S(1)}, f32[2,8,128]{2,1,0:T(8,128)S(1)}, u32[]{:S(2)}, u32[]{:S(2)}) collective-permute-start(f32[2,8,128]{2,1,0:T(8,128)S(1)} %pad_maximum_fusion.refs_0_), channel_id=1, source_target_pairs={{0,4},{1,5},{2,6},{3,7},{4,0},{5,1},{6,2},{7,3},{8,12},{9,13},{10,... | collective-permute-start | bytes 24584 | tf_op jit(solution)/shard_map/ppermute | solution.py:346
  38.4 5.4 %collective-permute-start.4 = (f32[2,8,128]{2,1,0:T(8,128)S(1)}, f32[2,8,128]{2,1,0:T(8,128)S(1)}, u32[]{:S(2)}, u32[]{:S(2)}) collective-permute-start(f32[2,8,128]{2,1,0:T(8,128)S(1)} %pad_maximum_fusion.refs_0_), channel_id=1, source_target_pairs={{0,2},{1,3},{2,4},{3,5},{4,6},{5,7},{6,0},{7,1},{8,10},{9,11},{10,... | collective-permute-start | bytes 24584 | tf_op jit(solution)/shard_map/ppermute | solution.py:346
  56.8 1.7 %collective-permute-start.9 = (f32[8,8,128]{2,1,0:T(8,128)S(1)}, f32[8,8,128]{2,1,0:T(8,128)S(1)}, u32[]{:S(2)}, u32[]{:S(2)}) collective-permute-start(f32[8,8,128]{2,1,0:T(8,128)S(1)} %get-tuple-element.10), channel_id=1, source_target_pairs={{0,24},{8,0},{16,8},{24,16},{1,25},{9,1},{17,9},{25,17},{2,26},{10... | collective-permute-start | bytes 98312 | tf_op jit(solution)/shard_map/ppermute | solution.py:346
  56.9 4.1 %collective-permute-start.8 = (f32[8,8,128]{2,1,0:T(8,128)S(1)}, f32[8,8,128]{2,1,0:T(8,128)S(1)}, u32[]{:S(2)}, u32[]{:S(2)}) collective-permute-start(f32[8,8,128]{2,1,0:T(8,128)S(1)} %get-tuple-element.10), channel_id=1, source_target_pairs={{0,16},{8,24},{16,0},{24,8},{1,17},{9,25},{17,1},{25,9},{2,18},{10... | collective-permute-start | bytes 98312 | tf_op jit(solution)/shard_map/ppermute | solution.py:346
  57.7 3.4 %collective-permute-start.7 = (f32[8,8,128]{2,1,0:T(8,128)S(1)}, f32[8,8,128]{2,1,0:T(8,128)S(1)}, u32[]{:S(2)}, u32[]{:S(2)}) collective-permute-start(f32[8,8,128]{2,1,0:T(8,128)S(1)} %get-tuple-element.10), channel_id=1, source_target_pairs={{0,8},{8,16},{16,24},{24,0},{1,9},{9,17},{17,25},{25,1},{2,10},{10... | collective-permute-start | bytes 98312 | tf_op jit(solution)/shard_map/ppermute | solution.py:346
  61.2 4.0 %collective-permute-start.10 = (f32[8,8,128]{2,1,0:T(8,128)S(1)}, f32[8,8,128]{2,1,0:T(8,128)S(1)}, u32[]{:S(2)}, u32[]{:S(2)}) collective-permute-start(f32[8,8,128]{2,1,0:T(8,128)S(1)} %add_add_fusion), channel_id=1, source_target_pairs={{0,1},{1,0},{2,3},{3,2},{4,5},{5,4},{6,7},{7,6},{8,9},{9,8},{10,11... | collective-permute-start | bytes 98312 | tf_op jit(solution)/shard_map/ppermute | solution.py:346
  65.2 3.9 %collective-permute-start.13 = (f32[8,8,128]{2,1,0:T(8,128)S(1)}, f32[8,8,128]{2,1,0:T(8,128)S(1)}, u32[]{:S(2)}, u32[]{:S(2)}) collective-permute-start(f32[8,8,128]{2,1,0:T(8,128)S(1)} %add.27.refs_0_), channel_id=1, source_target_pairs={{0,6},{1,7},{2,0},{3,1},{4,2},{5,3},{6,4},{7,5},{8,14},{9,15},{10,... | collective-permute-start | bytes 98312 | tf_op jit(solution)/shard_map/ppermute | solution.py:346
  66.6 5.2 %collective-permute-start.12 = (f32[8,8,128]{2,1,0:T(8,128)S(1)}, f32[8,8,128]{2,1,0:T(8,128)S(1)}, u32[]{:S(2)}, u32[]{:S(2)}) collective-permute-start(f32[8,8,128]{2,1,0:T(8,128)S(1)} %add.27.refs_0_), channel_id=1, source_target_pairs={{0,4},{1,5},{2,6},{3,7},{4,0},{5,1},{6,2},{7,3},{8,12},{9,13},{10,... | collective-permute-start | bytes 98312 | tf_op jit(solution)/shard_map/ppermute | solution.py:346
  67.4 5.7 %collective-permute-start.11 = (f32[8,8,128]{2,1,0:T(8,128)S(1)}, f32[8,8,128]{2,1,0:T(8,128)S(1)}, u32[]{:S(2)}, u32[]{:S(2)}) collective-permute-start(f32[8,8,128]{2,1,0:T(8,128)S(1)} %add.27.refs_0_), channel_id=1, source_target_pairs={{0,2},{1,3},{2,4},{3,5},{4,6},{5,7},{6,0},{7,1},{8,10},{9,11},{10,... | collective-permute-start | bytes 98312 | tf_op jit(solution)/shard_map/ppermute | solution.py:346
